TPU v7x, 32 devices: a whole 2x2x4 slice. The times are simulated.
32 devices in a mesh: dom: 8 (over z, x), sub: 4 (over y, core).
Axes of the slice: x: 2, y: 2, z: 4, core: 2. Of those that a mesh axis runs over, the one named last changes fastest.
Arguments:
- fine_residual: float32 [35, 5, 8192], P(None, None, ('dom', 'sub')), may hold values from -6 to 6
- fine_basis: float32 [64, 35], replicated, may hold values from -1 to 1
- coarse_basis: float32 [64, 10, 8192], P(None, None, ('dom', 'sub')), may hold values from -0.75 to 0.75
- donor_cells: int32 [8192, 4], P(('dom', 'sub')), may hold values from 0 to 4095, as said below
- point_counts: int32 [8192, 4], P(('dom', 'sub')), may hold values from 1 to 32, 64 in all within a row
- solver_pos: int32 [4096], P(('dom', 'sub')), may hold values from 0 to 4095, as said below
- block_inverse: float32 [50, 50, 4096], P(None, None, ('dom', 'sub')), may hold values from -0.25 to 1.65
- face_jacobian: float32 [4, 5, 5, 4096], P(None, None, None, ('dom', 'sub')), may hold values from -0.5 to 0.5
- face_lift: float32 [4, 10, 10], replicated, may hold values from -2 to 2
- face_offset: int32 [4, 4096], P(None, ('dom', 'sub')), may hold values from -32 to 32, as said below
Outputs:
- coarse_residual: float32 [50, 4096], P(None, ('dom', 'sub'))
- correction: float32 [50, 4096], P(None, ('dom', 'sub'))
Inputs may be any that keep to these rules, and one draw needn't show every extreme that they name: `donor_cells`: among the 4 donors of the 256 fine elements of one device, at most 64 lie in any one block of 128 consecutive coarse elements; in 1 group of 4 consecutive blocks every block receives exactly 64 from every device. `solver_pos`: A permutation; all 128 elements of one block go to one block of 128 solver positions in the same group of 4 consecutive blocks, distinct blocks to distinct ones. `face_offset`: 0 marks a boundary face, and so does a neighbour position outside 0 to 4095.
All inputs are finite; a program needn't handle non-finite values.
Results may differ from a plain program's by a relative error of at most 0.0003.
Values sent between devices are 32-bit elements; how exact they have to be, the bound alone decides.
No kernel may reach another device: no remote copies, remote signals or barrier semaphores. Data moves between devices by JAX's collectives and lax.ppermute only.
A program may use at most 64 MiB of HBM per device.

v0:
```python
import functools
import jax
import jax.numpy as jnp
from jax import lax
from jax.experimental import pallas as pl
from jax.experimental.pallas import tpu as pltpu
from jax.sharding import PartitionSpec as P

F32 = jnp.float32
BF16 = jnp.bfloat16
PLANE = ("low", "sub")
WHOLE = ("high", "low", "sub")
VMEM = pl.BlockSpec(memory_space=pltpu.VMEM)


def split(x):
    high = x.astype(BF16)
    return high, (x - high.astype(F32)).astype(BF16)


def mm(a, b, ca=1, cb=0, precision=None):
    return lax.dot_general(
        a, b, (((ca,), (cb,)), ((), ())), precision=precision, preferred_element_type=F32
    )


def rows_of(iota_shape, dim):
    return lax.broadcasted_iota(jnp.int32, iota_shape, dim)


def call(kernel, name, shapes, args, scratch=(), megabytes=8, cost=None, out_spec=VMEM):
    single = not isinstance(shapes, list)
    out = [jax.ShapeDtypeStruct(*shape) for shape in ([shapes] if single else shapes)]
    result = pl.pallas_call(
        kernel,
        out_shape=out,
        in_specs=[VMEM] * len(args),
        out_specs=[out_spec] * len(out),
        scratch_shapes=list(scratch),
        compiler_params=pltpu.CompilerParams(vmem_limit_bytes=megabytes * 2**20),
        cost_estimate=cost,
        name=name,
    )(*args)
    return result[0] if single else result


def swap_all(blocks, axis):
    count = len(blocks)
    return [blocks[0]] + [
        lax.ppermute(blocks[d], axis, [(i, i ^ d) for i in range(count)])
        for d in range(count - 1, 0, -1)
    ]


def constants_kernel(counter_ref):
    lanes = counter_ref.shape[0]
    earlier = (rows_of((lanes, lanes), 0) < rows_of((lanes, lanes), 1)).astype(F32)
    counter = jnp.concatenate([earlier, jnp.ones((lanes, lanes), F32)], axis=1)
    counter_ref[...] = counter.astype(BF16)


def free_columns(owner, counter, owners, passing, capacity, width, high):
    lanes = 128
    total = owner.shape[1]
    parts = total // lanes
    mine = (rows_of((owners, total), 0) == owner).astype(F32)
    stacked = jnp.concatenate([mine[:, j * lanes : (j + 1) * lanes] for j in range(parts)], axis=0)
    counted = mm(stacked.astype(BF16), counter)
    before = jnp.zeros((owners, lanes), F32)
    ranks = []
    for j in range(parts):
        own = mine[:, j * lanes : (j + 1) * lanes]
        part = counted[j * owners : (j + 1) * owners]
        ranks.append(jnp.sum(own * (before + part[:, :lanes]), axis=0, keepdims=True))
        before += part[:, lanes:]
    rank = jnp.concatenate(ranks, axis=1).astype(jnp.int32)
    return (owner % passing) * width + (owner // passing ^ high) * capacity + rank


def add_eights(x):
    total = x[0:8]
    for j in range(8, x.shape[0], 8):
        total += x[j : j + 8]
    return total


def sum_rows(pieces):
    row = rows_of(pieces[0].shape, 0)
    pieces = [pieces[k] for k in (3, 2, 1, 0, 7, 6, 5, 4)]
    upper = row < 4
    halves = []
    for one, two in zip(pieces[:4], pieces[4:]):
        kept, moved = jnp.where(upper, one, two), jnp.where(upper, two, one)
        halves.append(kept + pltpu.roll(moved, 4, 0))
    for shift in (2, 1):
        pairs = list(zip(halves[:shift], halves[shift:]))
        halves = [
            jnp.where(
                row & shift != 0, one + pltpu.roll(one, shift, 0), two + pltpu.roll(two, 8 - shift, 0)
            )
            for one, two in pairs
        ]
    return halves[0]


def restrict_kernel(
    counter_ref, res_ref, basis_ref, coarse_ref, counts_ref, donors_ref, out_hbm, pair_ref, out_ref, sems,
    *, owners, block, passing, capacity, few
):
    variables, _, fine = res_ref.shape
    modes, points, _ = coarse_ref.shape
    donors = counts_ref.shape[0]
    chunks = out_ref.shape[0]
    full = modes * variables
    depth = pair_ref.shape[1]
    total = donors * fine
    lanes = 128
    width = owners // passing * capacity

    cell = jnp.concatenate([donors_ref[k : k + 1, :] for k in range(donors)], axis=1)
    seat = (cell % block).astype(F32)
    for j in range(total // lanes):
        pair_ref[j, full:, :] = jnp.zeros((depth - full, lanes), F32)
        pair_ref[j, full : full + 1, :] = seat[:, j * lanes : (j + 1) * lanes]
    high = lax.axis_index("high") if few else 0
    slot = free_columns(cell // block, counter_ref[...], owners, passing, capacity, width, high)
    slot = jnp.broadcast_to(slot.astype(F32), (lanes, total)).T.astype(jnp.int32).astype(jnp.int16)

    basis_high, basis_low = split(basis_ref[...])
    res_high, res_low = split(jnp.concatenate([res_ref[v] for v in range(variables)], axis=1))
    values = mm(basis_high, res_high, 0, 0)
    values += mm(basis_high, res_low, 0, 0) + mm(basis_low, res_high, 0, 0)

    point = rows_of((points, lanes), 0)
    for at in range(0, fine, lanes):
        upper = jnp.zeros((1, lanes), jnp.int32)
        inside = []
        for k in range(donors):
            lower = upper
            upper = lower + counts_ref[k : k + 1, at : at + lanes]
            inside.append((point >= lower) & (point < upper))
        for v in range(variables):
            column = v * fine + at
            value = values[:, column : column + lanes]
            masked = [jnp.where(inside[k], value, 0.0) for k in range(donors)]
            pieces = []
            for a in range(modes):
                coarse = coarse_ref[a, :, at : at + lanes]
                terms = [coarse * masked[k] for k in range(donors)]
                pieces.append([add_eights(term) for term in terms])
            whole = modes - modes % 8
            for k in range(donors):
                left = k * fine + at
                for a in range(0, whole, 8):
                    rows = pl.ds(a * variables + v, 8, stride=variables)
                    pair_ref[left // lanes, rows, :] = sum_rows(
                        [pieces[a + r][k] for r in range(8)]
                    )
            rest = [(k, a) for k in range(donors) for a in range(whole, modes)]
            for first in range(0, len(rest), 8):
                group = rest[first : first + 8]
                filled = group + [group[0]] * (8 - len(group))
                sums = sum_rows([pieces[a][k] for k, a in filled])
                for r, (k, a) in enumerate(group):
                    row, left = a * variables + v, k * fine + at
                    pair_ref[left // lanes, row : row + 1, :] = sums[r : r + 1]

    pair = jnp.concatenate([pair_ref[j] for j in range(total // lanes)], axis=1)
    both = jnp.concatenate(split(pair), axis=0)
    lane = rows_of((total, lanes), 1).astype(jnp.int16)
    one, zero = jnp.ones((total, lanes), BF16), jnp.zeros((total, lanes), BF16)
    part = out_ref.shape[2]
    rows = out_ref.shape[1] * part // width
    together = max(1, 256 // width)
    for first in range(0, chunks, together):
        chooser = jnp.concatenate(
            [
                jnp.where(slot == lane + jnp.int16(first * width + j), one, zero)
                for j in range(0, together * width, lanes)
            ],
            axis=1,
        )
        placed = mm(both, chooser)
        placed = placed[:depth] + placed[depth:]
        for c in range(first, first + together):
            for j in range(width // part):
                at = (c - first) * width + j * part
                out_ref[c, j * rows : (j + 1) * rows] = placed[:rows, at : at + part]
            pltpu.make_async_copy(out_ref.at[c], out_hbm.at[c], sems.at[c]).start()
    for c in range(chunks):
        pltpu.make_async_copy(out_ref.at[c], out_hbm.at[c], sems.at[c]).wait()


def seat_kernel(columns_ref, *out_refs, groups, capacity, rows):
    sources = columns_ref.shape[0]
    full, block = out_refs[0].shape[-2:]
    for n, group in enumerate(groups):
        j, at = divmod(group * capacity, columns_ref.shape[2])
        got = jnp.concatenate(
            [
                columns_ref[s, j * rows : j * rows + full + 1, at : at + capacity]
                for s in range(sources)
            ],
            axis=1,
        )
        seat = got[full : full + 1, :]
        chooser = (rows_of((block, got.shape[1]), 0).astype(F32) == seat).astype(F32).astype(BF16)
        high, low = split(got)
        dense = (mm(high, chooser, 1, 1) + mm(low, chooser, 1, 1))[:full]
        if len(out_refs) == len(groups):
            out_refs[n][...] = dense
        else:
            out_refs[0][n] = dense


def renumber_kernel(place_ref, *refs):
    block_refs, out_ref = refs[:-1], refs[-1]
    block = place_ref.shape[1]
    if len(block_refs) == 1:
        total = block_refs[0][0]
        for h in range(1, block_refs[0].shape[0]):
            total += block_refs[0][h]
    else:
        total = block_refs[0][...]
        for ref in block_refs[1:]:
            total += ref[...]
    full = total.shape[0]
    place = place_ref[...]
    chooser = (rows_of((block, block), 0) == place % block).astype(F32).astype(BF16)
    high, low = split(total)
    out_ref[:full, :] = mm(high, chooser, 1, 1) + mm(low, chooser, 1, 1)
    out_ref[full:, :] = (place // block).astype(F32)


def prepare_kernel(after_ref, offset_ref, lift_ref, chooser_ref, lift_out_ref, *, variables, slab):
    del after_ref
    faces, block = offset_ref.shape
    modes = lift_ref.shape[0]
    full = modes * variables
    choose(offset_ref[...], chooser_ref, 0)
    width = variables * faces * slab
    column = rows_of((modes, width), 1)
    mode = rows_of((modes, width), 0)
    spread = jnp.zeros((modes, width), F32)
    for f in range(faces):
        put = (column % slab == mode) & ((column // slab) % faces == f)
        spread += mm(lift_ref[:, f, :], put.astype(F32), 1, 0, lax.Precision.HIGHEST)
    expand = (rows_of((full, modes), 0) // variables == rows_of((full, modes), 1)).astype(F32)
    lifted = mm(expand, spread, 1, 0, lax.Precision.HIGHEST)
    keep = rows_of((full, width), 1) // (slab * faces) == rows_of((full, width), 0) % variables
    high, low = split(jnp.where(keep, lifted, 0.0))
    lift_out_ref[...] = jnp.concatenate([high, high, low], axis=1)


def inner_is_left():
    return lax.axis_index("sub") % 2 == 1


def pack_quarters(pieces, for_left):
    reach = pieces[0].shape[1] // 4
    turned = [pieces[0]] + [pltpu.roll(pieces[g], g * reach, 1) for g in range(1, 4)]
    quarter = rows_of(pieces[0].shape, 1) // reach
    to_left, to_right = turned[0], turned[0]
    for g in range(1, 4):
        to_left = jnp.where(quarter == g, turned[g], to_left)
        to_right = jnp.where(quarter == g - 1, turned[g], to_right)
    return jnp.where(for_left, to_left, to_right)


def take_quarters(inner, outer):
    reach = inner.shape[1] // 4
    quarter = rows_of(inner.shape, 1) // reach
    pieces = []
    for g in range(4):
        piece = jnp.where((quarter == g) != inner_is_left(), inner, outer)
        pieces.append(pltpu.roll(piece, (4 - g) * reach, 1) if g else piece)
    return pieces


def pack_halves(one, two):
    block = one.shape[1]
    turned = pltpu.roll(two, block // 2, 1)
    kept = (rows_of(one.shape, 1) < block // 2) == inner_is_left()
    return jnp.where(kept, one, turned), jnp.where(kept, turned, one)


def take_halves(inner, outer):
    block = inner.shape[1]
    from_inner = (rows_of(inner.shape, 1) >= block // 2) == inner_is_left()
    two = jnp.where(from_inner, outer, inner)
    return jnp.where(from_inner, inner, outer), pltpu.roll(two, block // 2, 1)


def pack_kernel(after_ref, inverse_ref, jacobian_ref, offset_ref, out_ref, lines, *, outer):
    del after_ref
    full, _, block = inverse_ref.shape
    variables, _, faces, _ = jacobian_ref.shape
    for_left = inner_is_left() != outer
    slabs = -(-full // 4)
    for j in range(slabs):
        index = [j + g * slabs for g in range(4)]
        pieces = [inverse_ref[i] if i < full else jnp.zeros((full, block), F32) for i in index]
        out_ref[j * full : (j + 1) * full, :] = pack_quarters(pieces, for_left)
    for w in range(variables):
        for v in range(variables):
            at = (w * variables + v) * faces
            lines[at : at + faces, :] = jacobian_ref[w, v]
    count = lines.shape[0] // 4
    at, last = slabs * full, out_ref.shape[0] - faces
    pieces = [lines[g * count : (g + 1) * count, :] for g in range(4)]
    out_ref[at : at + count, :] = pack_quarters(pieces, for_left)
    out_ref[at + count : last, :] = jnp.zeros((last - at - count, block), F32)
    out_ref[last:, :] = offset_ref[...].astype(F32)


def beside_kernel(inner_ref, outer_ref, inverse_ref, jacobian_ref, chooser_ref, *, faces):
    full, _, block = inverse_ref.shape
    slabs = -(-full // 4)
    for j in range(slabs):
        at = j * full
        pieces = take_quarters(inner_ref[at : at + full, :], outer_ref[at : at + full, :])
        for g, piece in enumerate(pieces):
            if j + g * slabs < full:
                inverse_ref[j + g * slabs] = piece
    count = jacobian_ref.shape[0] // 4
    at = slabs * full
    pieces = take_quarters(inner_ref[at : at + count, :], outer_ref[at : at + count, :])
    for g, piece in enumerate(pieces):
        jacobian_ref[g * count : (g + 1) * count, :] = piece
    last = inner_ref.shape[0] - faces
    inner, outer = inner_ref[last:, :], outer_ref[last:, :]
    from_inner = (rows_of(inner.shape, 1) >= block // 2) == inner_is_left()
    choose(jnp.where(from_inner, inner, outer).astype(jnp.int32), chooser_ref, block)


def choose(offsets, chooser_ref, first):
    faces, block = offsets.shape
    lane = rows_of((1, block), 1) + first
    row = rows_of((2 * block, block), 0)
    for f in range(faces):
        offset = offsets[f : f + 1, :]
        source = jnp.where(offset != 0, (lane + offset) & (2 * block - 1), -1)
        chooser_ref[:, f * block : (f + 1) * block] = (row == source).astype(F32).astype(BF16)


def apply_inverse(inverse_ref, field, variables, depth=None):
    full, _, block = inverse_ref.shape
    modes = full // variables
    zero = jnp.zeros((8, block), F32)

    def piece(row):
        if row >= full:
            return zero
        product = inverse_ref[row % modes * variables + row // modes if depth else row] * field
        partial = product[0:8]
        for j in range(8, full - 7, 8):
            partial += product[j : j + 8]
        rest = full % 8
        if rest:
            partial += jnp.concatenate([product[full - rest :], zero[rest:]], axis=0)
        return partial

    rows = []
    for at in range(0, depth or full, 8):
        rows.append(sum_rows([piece(at + r) for r in range(8)]) if at < full else zero)
    return jnp.concatenate(rows, axis=0)[: depth or full]


def first_kernel(inverse_ref, *refs, subs, variables):
    block_refs, (total_ref, out_ref, inner_ref, outer_ref) = refs[:-4], refs[-4:]
    full = total_ref.shape[0]
    owner = lax.axis_index("high") * lax.axis_size("low") + lax.axis_index("low")
    owner = (owner * subs + lax.axis_index("sub")).astype(F32)
    residual = jnp.zeros(total_ref.shape, F32)
    for ref in block_refs:
        residual += jnp.where(ref[full:, :] == owner, ref[:full, :], 0.0)
    total_ref[...] = residual
    x = apply_inverse(inverse_ref, residual, variables, out_ref.shape[0])
    out_ref[...] = x
    half = inner_ref.shape[0]
    inner_ref[...], outer_ref[...] = pack_halves(x[:half], x[half:])


def sweep_kernel(
    inverse_ref, inverse_beside_ref, residual_ref, x_ref, outer_ref, inner_ref, chooser_ref,
    chooser_beside_ref, lift_ref, jacobian_ref, jacobian_beside_ref, total_ref, out_ref,
    picked_ref, z_ref, *, variables, slab
):
    depth, block = x_ref.shape
    full = residual_ref.shape[0]
    modes = full // variables
    faces = jacobian_ref.shape[2]
    residual = residual_ref[...]
    total_ref[...] = residual
    third = z_ref.shape[0] // 3

    def coupled(x, tiles):
        x = jnp.concatenate(split(x), axis=0)
        for t, ref in enumerate((chooser_ref, chooser_beside_ref)[:tiles]):
            picked = mm(x, ref[...])
            picked_ref[t] = picked[:depth] + picked[depth:]
        for t in range(tiles):
            for f in range(faces):
                at = f * block
                part = [
                    picked_ref[t, v * modes : v * modes + slab, at : at + block]
                    for v in range(variables)
                ]
                for w in range(variables):
                    z = None
                    for v in range(variables):
                        if t:
                            line = (w * variables + v) * faces + f
                            term = part[v] * jacobian_beside_ref[line : line + 1, :]
                        else:
                            term = part[v] * jacobian_ref[w, v, f : f + 1, :]
                        z = z + term if v else term
                    line, column = (w * faces + f) * slab, t * block
                    high, low = split(z)
                    for n, value in enumerate((high, low, high)):
                        at_row = n * third + line
                        z_ref[at_row : at_row + slab, column : column + block] = value
        return mm(lift_ref[...], z_ref[:, : tiles * block])

    first = x_ref[...]
    first_beside = jnp.concatenate(take_halves(inner_ref[...], outer_ref[...]), axis=0)
    taken = coupled(jnp.concatenate([first, first_beside], axis=1), 2)
    second = jnp.concatenate(
        [
            first - apply_inverse(inverse_ref, taken[:, :block], variables, depth),
            first_beside - apply_inverse(inverse_beside_ref, taken[:, block:], variables, depth),
        ],
        axis=1,
    )
    out_ref[...] = apply_inverse(inverse_ref, residual - coupled(second, 1), variables)


def per_device(
    fine_residual,
    fine_basis,
    coarse_basis,
    donor_cells,
    point_counts,
    solver_pos,
    block_inverse,
    face_jacobian,
    face_lift,
    face_offset,
):
    high_count = lax.axis_size("high")
    passing = lax.axis_size("low") * lax.axis_size("sub")
    owners = high_count * passing
    _, variables, fine = fine_residual.shape
    modes = coarse_basis.shape[1]
    donors = donor_cells.shape[1]
    block = solver_pos.shape[0]
    faces = face_offset.shape[0]
    full = modes * variables
    slab = -(-modes // 16) * 16
    depth = -(-full // 16) * 16

    capacity = max(2, 2 * fine * donors // owners)
    few = 1 < high_count <= 8 and high_count & (high_count - 1) == 0
    subs = lax.axis_size("sub")
    counter = call(
        constants_kernel,
        "constants",
        ((128, 256), BF16),
        (),
        cost=pl.CostEstimate(flops=2 * 10**9, bytes_accessed=8 * 10**6, transcendentals=0),
    )
    width = high_count * capacity
    halves = 2 if width > 128 else 1
    rows = -(-(full + 1) // 4) * 4 if halves > 1 else -(-(full + 1) // 8) * 8
    chunk_shape = (passing, halves * rows, width // halves)
    columns = call(
        functools.partial(
            restrict_kernel,
            owners=owners,
            block=block,
            passing=passing,
            capacity=capacity,
            few=few,
        ),
        "restrict",
        (chunk_shape, F32),
        (
            counter,
            fine_residual.transpose(1, 0, 2),
            fine_basis.T,
            coarse_basis.transpose(1, 0, 2),
            point_counts.T,
            donor_cells.T,
        ),
        [
            pltpu.VMEM((donors * fine // 128, depth, 128), F32),
            pltpu.VMEM(chunk_shape, F32),
            pltpu.SemaphoreType.DMA((passing,)),
        ],
        megabytes=16,
        out_spec=pl.BlockSpec(memory_space=pl.ANY),
    )
    columns = lax.all_to_all(columns, PLANE, 0, 0, tiled=True)
    def seat(name, groups, shapes):
        return call(
            functools.partial(seat_kernel, groups=groups, capacity=capacity, rows=rows),
            name,
            shapes,
            (columns,),
            megabytes=24,
        )

    dense = ((full, block), F32)
    if few:
        count = high_count // 2
        near = seat("seat_near", range(count), [dense] * count)
        rest = [seat("seat_far", [d], [dense])[0] for d in range(count, high_count)]
        blocks = swap_all([*near, *rest], "high")
    else:
        blocks = seat("seat_all", range(high_count), ((high_count, full, block), F32))
        blocks = [lax.all_to_all(blocks, "high", 0, 0, tiled=True)]
    whole = call(
        renumber_kernel, "renumber", ((full + 1, block), F32), (solver_pos[None, :], *blocks)
    )
    blocks = swap_all([whole] * subs, "sub")

    jacobian = face_jacobian.transpose(1, 2, 0, 3)
    chooser, lift = call(
        functools.partial(prepare_kernel, variables=variables, slab=slab),
        "prepare",
        [((2 * block, faces * block), BF16), ((full, 3 * variables * faces * slab), BF16)],
        (counter, face_offset, face_lift.transpose(1, 0, 2)),
    )
    outer_pairs = [(i, i + 1) for i in range(1, owners - 1, 2)]
    outer_pairs += [(j, i) for i, j in outer_pairs]
    inner_pairs = [(i, i ^ 1) for i in range(owners)]
    lines = variables * variables * faces
    packed = ((-(-(-(-full // 4) * full + lines // 4 + faces + 1) // 8) * 8, block), F32)
    packs = []
    for outer in (False, True):
        packs.append(
            call(
                functools.partial(pack_kernel, outer=outer),
                "pack_outer" if outer else "pack_inner",
                packed,
                (packs[0] if outer else lift, block_inverse, jacobian, face_offset),
                [pltpu.VMEM((lines, block), F32)],
            )
        )
    inner = lax.ppermute(packs[0], WHOLE, inner_pairs)
    outer = lax.ppermute(packs[1], WHOLE, outer_pairs)
    inverse_beside, jacobian_beside, chooser_beside = call(
        functools.partial(beside_kernel, faces=faces),
        "beside",
        [((full, full, block), F32), ((lines, block), F32), ((2 * block, faces * block), BF16)],
        (inner, outer),
    )
    plain, edge = ((full, block), F32), ((depth // 2, block), F32)
    residual, x, to_inner, to_outer = call(
        functools.partial(first_kernel, subs=subs, variables=variables),
        "first",
        [plain, ((depth, block), F32), edge, edge],
        (block_inverse, *blocks),
    )
    outer = lax.ppermute(to_outer, WHOLE, outer_pairs)
    inner = lax.ppermute(to_inner, WHOLE, inner_pairs)
    return tuple(
        call(
            functools.partial(sweep_kernel, variables=variables, slab=slab),
            "sweeps",
            [plain, plain],
            (
                block_inverse,
                inverse_beside,
                residual,
                x,
                outer,
                inner,
                chooser,
                chooser_beside,
                lift,
                jacobian,
                jacobian_beside,
            ),
            [pltpu.VMEM((2, depth, faces * block), F32)]
            + [pltpu.VMEM((3 * variables * faces * slab, 2 * block), BF16)],
        )
    )


def solution(mesh):
    dom, sub = mesh.devices.shape
    low = next(count for count in (4, 2, 1) if dom % count == 0)
    split_mesh = jax.sharding.Mesh(mesh.devices.reshape(dom // low, low, sub), WHOLE)
    in_specs = (
        P(None, None, WHOLE),
        P(),
        P(None, None, WHOLE),
        P(WHOLE, None),
        P(WHOLE, None),
        P(WHOLE),
        P(None, None, WHOLE),
        P(None, None, None, WHOLE),
        P(),
        P(None, WHOLE),
    )
    return jax.shard_map(
        per_device,
        mesh=split_mesh,
        in_specs=in_specs,
        out_specs=(P(None, WHOLE), P(None, WHOLE)),
        check_vma=False,
    )
```

profile of v0, /device:TPU:16, one launch (start us, length us, event | category | flops | bytes accessed | tf_op | source)
XLA Modules:
  0.0 39.1 jit_solution(10074573918888468098)
XLA Ops:
  0.6 0.0 copy-start.9
  0.6 0.0 copy-start.10
  0.7 0.0 copy-start.1
  0.7 0.0 copy-start.7
  0.7 0.0 copy-start.5
  0.7 0.0 copy-start.6
  0.7 0.0 copy-start.8
  0.7 0.0 copy-start
  0.7 0.0 copy-start.2
  0.8 0.6 %copy-done.9 = s32[256,4]{0,1:T(4,128)S(1)} copy-done((s32[256,4]{0,1:T(4,128)S(1)}, s32[256,4]{0,1:T(4,128)}, u32[]{:S(2)}) %copy-start.9) | copy-done | bytes 4120
  1.3 0.0 copy-done.10
  1.3 0.4 %copy-done.1 = f32[64,10,256]{2,0,1:T(8,128)S(1)} copy-done((f32[64,10,256]{2,0,1:T(8,128)S(1)}, f32[64,10,256]{2,0,1:T(8,128)}, u32[]{:S(2)}) %copy-start.1) | copy-done | bytes 655384
  1.8 0.0 copy-done.7
  1.8 0.1 copy-done.5
  1.8 3.2 %restrict.1 = f32[16,56,128]{2,1,0:T(8,128)} custom-call(bf16[128,256]{1,0:T(8,128)(2,1)S(1)} %constants.1.after_ref.counter_ref, f32[5,35,256]{2,1,0:T(8,128)S(1)} %bitcast.12, f32[35,64]{1,0:T(8,128)S(1)} %bitcast.14, f32[10,64,256]{2,1,0:T(8,128)S(1)} %bitcast.8, s32[4,256]{1,0:T(4,128)S(1)} %bitcast.15, s32[4,256]{1,0:T(4,128)S(1)} %bitcast.16), custom_call_target="tpu_custom_call" | custom-call | tf_op jit(solution)/shard_map/restrict/pallas_call | solution.py:34
  5.1 4.9 %all-to-all-start = ((f32[16,56,128]{2,1,0:T(8,128)}), f32[16,56,128]{2,1,0:T(8,128)S(1)}, u32[]{:S(2)}, u32[]{:S(2)}) async-start(f32[16,56,128]{2,1,0:T(8,128)} %restrict.1), calls=%async_computation | async-start | bytes 917504 | tf_op jit(solution)/shard_map/all_to_all | solution.py:503
  9.9 0.0 copy-done.6
  9.9 0.0 copy-done.8
  9.9 0.7 %prepare.1 = (bf16[256,512]{1,0:T(8,128)(2,1)S(1)}, bf16[50,960]{1,0:T(8,128)(2,1)S(1)}) custom-call(bf16[128,256]{1,0:T(8,128)(2,1)S(1)} %constants.1.after_ref.counter_ref, s32[4,128]{1,0:T(4,128)S(1)} %copy-done.8, f32[10,4,10]{2,1,0:T(4,128)S(1)} %bitcast.13), custom_call_target="tpu_custom_call" | custom-call | tf_op jit(solution)/shard_map/prepare/pallas_call | solution.py:34
  10.6 0.7 %copy-done.3 = bf16[256,512]{1,0:T(8,128)(2,1)} copy-done((bf16[256,512]{1,0:T(8,128)(2,1)}, bf16[256,512]{1,0:T(8,128)(2,1)S(1)}, u32[]{:S(2)}) %copy-start.3) | copy-done | bytes 262168
  11.4 0.4 pack_inner.1.after_ref
  11.7 0.0 copy-start.11
  11.7 0.4 pack_outer.1
  12.1 4.3 %collective-permute-start.1 = (f32[680,128]{1,0:T(8,128)S(1)}, f32[680,128]{1,0:T(8,128)S(1)}, u32[]{:S(2)}, u32[]{:S(2)}) collective-permute-start(f32[680,128]{1,0:T(8,128)S(1)} %pack_outer.1), channel_id=1, source_target_pairs={{1,2},{3,4},{5,6},{7,8},{9,10},{11,12},{13,14},{15,16},{17,18},{19... | collective-permute-start | bytes 1044488 | tf_op jit(solution)/shard_map/ppermute | solution.py:551
  16.4 0.1 collective-permute-start
  16.4 4.0 %all-to-all-done.columns_ref = f32[16,56,128]{2,1,0:T(8,128)S(1)} async-done(((f32[16,56,128]{2,1,0:T(8,128)}), f32[16,56,128]{2,1,0:T(8,128)S(1)}, u32[]{:S(2)}, u32[]{:S(2)}) %all-to-all-start) | async-done | bytes 458784 | tf_op jit(solution)/shard_map/all_to_all | solution.py:503
  20.4 0.4 seat_far.1
  20.8 0.0 copy-start.4
  20.8 0.1 collective-permute-start.2
  20.9 0.4 seat_near.1.refs_0_
  21.3 4.4 %collective-permute-done.2.refs_1_ = f32[50,128]{1,0:T(8,128)S(1)} collective-permute-done((f32[50,128]{1,0:T(8,128)S(1)}, f32[50,128]{1,0:T(8,128)S(1)}, u32[]{:S(2)}, u32[]{:S(2)}) %collective-permute-start.2) | collective-permute-done | bytes 25632 | tf_op jit(solution)/shard_map/ppermute | solution.py:50
  25.6 0.0 copy-done.11
  25.7 0.1 renumber.1.refs_0_
  25.8 0.0 collective-permute-start.5
  25.8 0.1 collective-permute-start.4
  25.9 1.8 %collective-permute-start.3 = (f32[51,128]{1,0:T(8,128)S(1)}, f32[51,128]{1,0:T(8,128)S(1)}, u32[]{:S(2)}, u32[]{:S(2)}) collective-permute-start(f32[51,128]{1,0:T(8,128)S(1)} %renumber.1.refs_0_), channel_id=1, source_target_pairs={{0,3},{1,2},{2,1},{3,0},{4,7},{5,6},{6,5},{7,4},{8,11},{9,10},{10,... | collective-permute-start | bytes 78344 | tf_op jit(solution)/shard_map/ppermute | solution.py:50
  27.7 0.0 collective-permute-done.5.refs_3_
  27.7 2.2 %collective-permute-done.4.refs_2_ = f32[51,128]{1,0:T(8,128)S(1)} collective-permute-done((f32[51,128]{1,0:T(8,128)S(1)}, f32[51,128]{1,0:T(8,128)S(1)}, u32[]{:S(2)}, u32[]{:S(2)}) %collective-permute-start.4) | collective-permute-done | bytes 26144 | tf_op jit(solution)/shard_map/ppermute | solution.py:50
  29.8 0.0 collective-permute-done.3.refs_1_
  29.8 0.1 first.1
  30.0 1.9 %collective-permute-start.6 = (f32[32,128]{1,0:T(8,128)S(1)}, f32[32,128]{1,0:T(8,128)S(1)}, u32[]{:S(2)}, u32[]{:S(2)}) collective-permute-start(f32[32,128]{1,0:T(8,128)S(1)} %get-tuple-element.15), channel_id=1, source_target_pairs={{1,2},{3,4},{5,6},{7,8},{9,10},{11,12},{13,14},{15,16},{17,18},{19... | collective-permute-start | bytes 49160 | tf_op jit(solution)/shard_map/ppermute | solution.py:565
  31.9 1.5 %collective-permute-start.7 = (f32[32,128]{1,0:T(8,128)S(1)}, f32[32,128]{1,0:T(8,128)S(1)}, u32[]{:S(2)}, u32[]{:S(2)}) collective-permute-start(f32[32,128]{1,0:T(8,128)S(1)} %get-tuple-element.16), channel_id=1, source_target_pairs={{0,1},{1,0},{2,3},{3,2},{4,5},{5,4},{6,7},{7,6},{8,9},{9,8},{10,11... | collective-permute-start | bytes 49160 | tf_op jit(solution)/shard_map/ppermute | solution.py:566
  33.5 0.0 collective-permute-done.1.outer_ref
  33.5 0.0 collective-permute-done.inner_ref
  33.5 0.4 %beside.1 = (f32[50,50,128]{2,1,0:T(8,128)S(1)}, f32[100,128]{1,0:T(8,128)S(1)}, bf16[256,512]{1,0:T(8,128)(2,1)S(1)}) custom-call(f32[680,128]{1,0:T(8,128)S(1)} %collective-permute-done.inner_ref, f32[680,128]{1,0:T(8,128)S(1)} %collective-permute-done.1.outer_ref), custom_call_target="tpu_custom_call" | custom-call | tf_op jit(solution)/shard_map/beside/pallas_call | solution.py:34
  33.9 3.0 %collective-permute-done.6.outer_ref = f32[32,128]{1,0:T(8,128)S(1)} collective-permute-done((f32[32,128]{1,0:T(8,128)S(1)}, f32[32,128]{1,0:T(8,128)S(1)}, u32[]{:S(2)}, u32[]{:S(2)}) %collective-permute-start.6) | collective-permute-done | bytes 16416 | tf_op jit(solution)/shard_map/ppermute | solution.py:565
  36.9 0.0 collective-permute-done.7.inner_ref
  36.9 2.2 %sweeps.1 = (f32[50,128]{1,0:T(8,128)}, f32[50,128]{1,0:T(8,128)}) custom-call(f32[50,50,128]{2,1,0:T(8,128)S(1)} %copy-done, f32[50,50,128]{2,1,0:T(8,128)S(1)} %get-tuple-element.12.inverse_beside_ref, f32[50,128]{1,0:T(8,128)S(1)} %get-tuple-element.13.residual_ref, f32[64,128]{1,0:T(8,128)S(1)} %get-tuple-element.14.x_ref, ...), custom_call_target="tpu_custom_call" | custom-call | tf_op jit(solution)/shard_map/sweeps/pallas_call | solution.py:34
  (5 shorter events, 0.0 us)
Async XLA Ops:
  0.6 0.7 %copy-start.9 = (s32[256,4]{0,1:T(4,128)S(1)}, s32[256,4]{0,1:T(4,128)}, u32[]{:S(2)}) copy-start(s32[256,4]{0,1:T(4,128)} %param.14) | copy-start | bytes 12292
  0.6 0.7 %copy-start.10 = (s32[256,4]{0,1:T(4,128)S(1)}, s32[256,4]{0,1:T(4,128)}, u32[]{:S(2)}) copy-start(s32[256,4]{0,1:T(4,128)} %param.13) | copy-start | bytes 12292
  0.7 1.1 %copy-start.1 = (f32[64,10,256]{2,0,1:T(8,128)S(1)}, f32[64,10,256]{2,0,1:T(8,128)}, u32[]{:S(2)}) copy-start(f32[64,10,256]{2,0,1:T(8,128)} %param.12) | copy-start | bytes 1966084
  0.7 1.1 %copy-start.7 = (f32[64,35]{0,1:T(8,128)S(1)}, f32[64,35]{0,1:T(8,128)}, u32[]{:S(2)}) copy-start(f32[64,35]{0,1:T(8,128)} %param.11) | copy-start | bytes 26884
  0.7 1.1 %copy-start.5 = (f32[35,5,256]{2,0,1:T(8,128)S(1)}, f32[35,5,256]{2,0,1:T(8,128)}, u32[]{:S(2)}) copy-start(f32[35,5,256]{2,0,1:T(8,128)} %param.10) | copy-start | bytes 537604
  0.7 9.2 %copy-start.6 = (f32[4,10,10]{2,0,1:T(4,128)S(1)}, f32[4,10,10]{2,0,1:T(4,128)}, u32[]{:S(2)}) copy-start(f32[4,10,10]{2,0,1:T(4,128)} %param.18) | copy-start | bytes 4804
  0.7 9.2 %copy-start.8 = (s32[4,128]{1,0:T(4,128)S(1)}, s32[4,128]{1,0:T(4,128)}, u32[]{:S(2)}) copy-start(s32[4,128]{1,0:T(4,128)} %offset_ref.5) | copy-start | bytes 6148
  0.7 10.6 %copy-start = (f32[50,50,128]{2,1,0:T(8,128)S(1)}, f32[50,50,128]{2,1,0:T(8,128)}, u32[]{:S(2)}) copy-start(f32[50,50,128]{2,1,0:T(8,128)} %inverse_ref.7) | copy-start | bytes 3840004
  0.7 10.6 %copy-start.2 = (f32[4,5,5,128]{3,0,2,1:T(4,128)S(1)}, f32[4,5,5,128]{3,0,2,1:T(4,128)}, u32[]{:S(2)}) copy-start(f32[4,5,5,128]{3,0,2,1:T(4,128)} %param.17) | copy-start | bytes 153604
  5.1 15.4 %all-to-all-start = ((f32[16,56,128]{2,1,0:T(8,128)}), f32[16,56,128]{2,1,0:T(8,128)S(1)}, u32[]{:S(2)}, u32[]{:S(2)}) async-start(f32[16,56,128]{2,1,0:T(8,128)} %restrict.1), calls=%async_computation | async-start | bytes 917504 | tf_op jit(solution)/shard_map/all_to_all | solution.py:503
  10.6 0.7 %copy-start.3 = (bf16[256,512]{1,0:T(8,128)(2,1)}, bf16[256,512]{1,0:T(8,128)(2,1)S(1)}, u32[]{:S(2)}) copy-start(bf16[256,512]{1,0:T(8,128)(2,1)S(1)} %get-tuple-element.17.chooser_ref) | copy-start | bytes 786436
  11.7 13.9 %copy-start.11 = (s32[128]{0:T(128)S(1)}, s32[128]{0:T(128)}, u32[]{:S(2)}) copy-start(s32[128]{0:T(128)} %param.15) | copy-start | bytes 1540
  12.1 21.4 %collective-permute-start.1 = (f32[680,128]{1,0:T(8,128)S(1)}, f32[680,128]{1,0:T(8,128)S(1)}, u32[]{:S(2)}, u32[]{:S(2)}) collective-permute-start(f32[680,128]{1,0:T(8,128)S(1)} %pack_outer.1), channel_id=1, source_target_pairs={{1,2},{3,4},{5,6},{7,8},{9,10},{11,12},{13,14},{15,16},{17,18},{19... | collective-permute-start | bytes 1044488 | tf_op jit(solution)/shard_map/ppermute | solution.py:551
  16.4 17.1 %collective-permute-start = (f32[680,128]{1,0:T(8,128)S(1)}, f32[680,128]{1,0:T(8,128)S(1)}, u32[]{:S(2)}, u32[]{:S(2)}) collective-permute-start(f32[680,128]{1,0:T(8,128)S(1)} %pack_inner.1.after_ref), channel_id=1, source_target_pairs={{0,1},{1,0},{2,3},{3,2},{4,5},{5,4},{6,7},{7,6},{8,9},{9,8},{10,11... | collective-permute-start | bytes 1044488 | tf_op jit(solution)/shard_map/ppermute | solution.py:550
  20.8 16.1 %copy-start.4 = (bf16[256,512]{1,0:T(8,128)(2,1)S(1)}, bf16[256,512]{1,0:T(8,128)(2,1)}, u32[]{:S(2)}) copy-start(bf16[256,512]{1,0:T(8,128)(2,1)} %copy-done.3) | copy-start | bytes 786436
  20.8 4.8 %collective-permute-start.2 = (f32[50,128]{1,0:T(8,128)S(1)}, f32[50,128]{1,0:T(8,128)S(1)}, u32[]{:S(2)}, u32[]{:S(2)}) collective-permute-start(f32[50,128]{1,0:T(8,128)S(1)} %seat_far.1), channel_id=1, source_target_pairs={{0,16},{16,0},{1,17},{17,1},{2,18},{18,2},{3,19},{19,3},{4,20},{20... | collective-permute-start | bytes 76808 | tf_op jit(solution)/shard_map/ppermute | solution.py:50
  25.8 1.9 %collective-permute-start.5 = (f32[51,128]{1,0:T(8,128)S(1)}, f32[51,128]{1,0:T(8,128)S(1)}, u32[]{:S(2)}, u32[]{:S(2)}) collective-permute-start(f32[51,128]{1,0:T(8,128)S(1)} %renumber.1.refs_0_), channel_id=1, source_target_pairs={{0,1},{1,0},{2,3},{3,2},{4,5},{5,4},{6,7},{7,6},{8,9},{9,8},{10,11... | collective-permute-start | bytes 78344 | tf_op jit(solution)/shard_map/ppermute | solution.py:50
  25.8 4.0 %collective-permute-start.4 = (f32[51,128]{1,0:T(8,128)S(1)}, f32[51,128]{1,0:T(8,128)S(1)}, u32[]{:S(2)}, u32[]{:S(2)}) collective-permute-start(f32[51,128]{1,0:T(8,128)S(1)} %renumber.1.refs_0_), channel_id=1, source_target_pairs={{0,2},{1,3},{2,0},{3,1},{4,6},{5,7},{6,4},{7,5},{8,10},{9,11},{10,... | collective-permute-start | bytes 78344 | tf_op jit(solution)/shard_map/ppermute | solution.py:50
  25.9 3.9 %collective-permute-start.3 = (f32[51,128]{1,0:T(8,128)S(1)}, f32[51,128]{1,0:T(8,128)S(1)}, u32[]{:S(2)}, u32[]{:S(2)}) collective-permute-start(f32[51,128]{1,0:T(8,128)S(1)} %renumber.1.refs_0_), channel_id=1, source_target_pairs={{0,3},{1,2},{2,1},{3,0},{4,7},{5,6},{6,5},{7,4},{8,11},{9,10},{10,... | collective-permute-start | bytes 78344 | tf_op jit(solution)/shard_map/ppermute | solution.py:50
  30.0 6.9 %collective-permute-start.6 = (f32[32,128]{1,0:T(8,128)S(1)}, f32[32,128]{1,0:T(8,128)S(1)}, u32[]{:S(2)}, u32[]{:S(2)}) collective-permute-start(f32[32,128]{1,0:T(8,128)S(1)} %get-tuple-element.15), channel_id=1, source_target_pairs={{1,2},{3,4},{5,6},{7,8},{9,10},{11,12},{13,14},{15,16},{17,18},{19... | collective-permute-start | bytes 49160 | tf_op jit(solution)/shard_map/ppermute | solution.py:565
  31.9 4.9 %collective-permute-start.7 = (f32[32,128]{1,0:T(8,128)S(1)}, f32[32,128]{1,0:T(8,128)S(1)}, u32[]{:S(2)}, u32[]{:S(2)}) collective-permute-start(f32[32,128]{1,0:T(8,128)S(1)} %get-tuple-element.16), channel_id=1, source_target_pairs={{0,1},{1,0},{2,3},{3,2},{4,5},{5,4},{6,7},{7,6},{8,9},{9,8},{10,11... | collective-permute-start | bytes 49160 | tf_op jit(solution)/shard_map/ppermute | solution.py:566
where the time goes:
time: 39.3 us; the launch traced here: 39.1 us
  starting transfers between devices  14.6 us (37%)
  waiting for transfers between devices  13.5 us (34%)
  Pallas kernels  8.31 us (21%)
  local copies, waits for them, and re-layouts  1.81 us (5%)
  between operations  0.86 us (2%)
    pallas_call x11, Pallas kernels, call(): pl.pallas_call(kernel, out_shape=out, in_specs=[VMEM] * len(args), out_sp...  8.31 us
    ppermute x4, waiting for transfers between devices, swap_all(): lax.ppermute(blocks[d], axis, [(i, i ^ d) for i in range(count)])  6.55 us
    all_to_all x1, starting transfers between devices, per_device(): columns = lax.all_to_all(columns, PLANE, 0, 0, tiled=True)  4.85 us
    ppermute x1, starting transfers between devices, per_device(): outer = lax.ppermute(packs[1], WHOLE, outer_pairs)  4.26 us
    all_to_all x1, waiting for transfers between devices, per_device(): columns = lax.all_to_all(columns, PLANE, 0, 0, tiled=True)  3.99 us
    ppermute x1, waiting for transfers between devices, per_device(): outer = lax.ppermute(to_outer, WHOLE, outer_pairs)  2.96 us
    ppermute x4, starting transfers between devices, swap_all(): lax.ppermute(blocks[d], axis, [(i, i ^ d) for i in range(count)])  1.94 us
    ppermute x1, starting transfers between devices, per_device(): outer = lax.ppermute(to_outer, WHOLE, outer_pairs)  1.92 us
  transfers between devices with their start and end apart: 9, of which 4 were waited for; matrix products, arithmetic and copies ran while one was open for 0% of the time, Pallas kernels for 7%

commit v1 on v0

--- a/solution.py
+++ b/solution.py
@@ -8,7 +8,7 @@
 
 F32 = jnp.float32
 BF16 = jnp.bfloat16
-PLANE = ("low", "sub")
+PLANE = ("sub", "low")
 WHOLE = ("high", "low", "sub")
 VMEM = pl.BlockSpec(memory_space=pltpu.VMEM)
 
@@ -59,7 +59,7 @@
     counter_ref[...] = counter.astype(BF16)
 
 
-def free_columns(owner, counter, owners, passing, capacity, width, high):
+def free_columns(owner, counter, owners, passing, subs, capacity, width, high):
     lanes = 128
     total = owner.shape[1]
     parts = total // lanes
@@ -74,7 +74,9 @@
         ranks.append(jnp.sum(own * (before + part[:, :lanes]), axis=0, keepdims=True))
         before += part[:, lanes:]
     rank = jnp.concatenate(ranks, axis=1).astype(jnp.int32)
-    return (owner % passing) * width + (owner // passing ^ high) * capacity + rank
+    lows = passing // subs
+    chunk = owner % subs * lows + owner // subs % lows
+    return chunk * width + (owner // passing ^ high) * capacity + rank
 
 
 def add_eights(x):
@@ -105,7 +107,7 @@
 
 def restrict_kernel(
     counter_ref, res_ref, basis_ref, coarse_ref, counts_ref, donors_ref, out_hbm, pair_ref, out_ref, sems,
-    *, owners, block, passing, capacity, few
+    *, owners, block, passing, subs, capacity, few
 ):
     variables, _, fine = res_ref.shape
     modes, points, _ = coarse_ref.shape
@@ -123,7 +125,8 @@
         pair_ref[j, full:, :] = jnp.zeros((depth - full, lanes), F32)
         pair_ref[j, full : full + 1, :] = seat[:, j * lanes : (j + 1) * lanes]
     high = lax.axis_index("high") if few else 0
-    slot = free_columns(cell // block, counter_ref[...], owners, passing, capacity, width, high)
+    owner = cell // block
+    slot = free_columns(owner, counter_ref[...], owners, passing, subs, capacity, width, high)
     slot = jnp.broadcast_to(slot.astype(F32), (lanes, total)).T.astype(jnp.int32).astype(jnp.int16)
 
     basis_high, basis_low = split(basis_ref[...])
@@ -479,6 +482,7 @@
             owners=owners,
             block=block,
             passing=passing,
+            subs=subs,
             capacity=capacity,
             few=few,
         ),

time: 39.3 us -> 38.7 us (0.985)
  waiting for transfers between devices: 13.5 us -> 13.1 us
    all_to_all x1, waiting for transfers between devices: 3.99 us -> 2.12 us  [per_device(): columns = lax.all_to_all(columns, PLANE, 0, 0, tiled=True)]
    ppermute x4, waiting for transfers between devices: 6.55 us -> 7.28 us  [swap_all(): lax.ppermute(blocks[d], axis, [(i, i ^ d) for i in range(count)])]
    ppermute x1, starting transfers between devices: 1.52 us -> 0.84 us  [per_device(): inner = lax.ppermute(to_inner, WHOLE, inner_pairs)]
    ppermute x1, waiting for transfers between devices: 2.96 us -> 3.65 us  [per_device(): outer = lax.ppermute(to_outer, WHOLE, outer_pairs)]
    ppermute x4, starting transfers between devices: 1.94 us -> 2.45 us  [swap_all(): lax.ppermute(blocks[d], axis, [(i, i ^ d) for i in range(count)])]
  transfers between devices with their start and end apart: 9 -> 9, of which waited for: 4 -> 5; matrix products, arithmetic and copies ran while one was open for 0% -> 0% of each run, Pallas kernels for 7% -> 7%
where the time goes in v1:
time: 38.7 us; the launch traced here: 38.4 us
  starting transfers between devices  14.4 us (37%)
  waiting for transfers between devices  13.1 us (34%)
  Pallas kernels  8.32 us (21%)
  local copies, waits for them, and re-layouts  1.81 us (5%)
  between operations  0.84 us (2%)
    pallas_call x11, Pallas kernels, call(): pl.pallas_call(kernel, out_shape=out, in_specs=[VMEM] * len(args), out_sp...  8.32 us
    ppermute x4, waiting for transfers between devices, swap_all(): lax.ppermute(blocks[d], axis, [(i, i ^ d) for i in range(count)])  7.28 us
    all_to_all x1, starting transfers between devices, per_device(): columns = lax.all_to_all(columns, PLANE, 0, 0, tiled=True)  4.85 us
    ppermute x1, starting transfers between devices, per_device(): outer = lax.ppermute(packs[1], WHOLE, outer_pairs)  4.26 us
    ppermute x1, waiting for transfers between devices, per_device(): outer = lax.ppermute(to_outer, WHOLE, outer_pairs)  3.65 us
    ppermute x4, starting transfers between devices, swap_all(): lax.ppermute(blocks[d], axis, [(i, i ^ d) for i in range(count)])  2.45 us
    all_to_all x1, waiting for transfers between devices, per_device(): columns = lax.all_to_all(columns, PLANE, 0, 0, tiled=True)  2.12 us
    ppermute x1, starting transfers between devices, per_device(): outer = lax.ppermute(to_outer, WHOLE, outer_pairs)  1.92 us
  transfers between devices with their start and end apart: 9, of which 5 were waited for; matrix products, arithmetic and copies ran while one was open for 0% of the time, Pallas kernels for 7%

profile of v1, /device:TPU:16, one launch (start us, length us, event | category | flops | bytes accessed | tf_op | source)
XLA Modules:
  0.0 38.4 jit_solution(9976219108415542866)
XLA Ops:
  0.6 0.0 copy-start.9
  0.6 0.0 copy-start.10
  0.7 0.0 copy-start.1
  0.7 0.0 copy-start.7
  0.7 0.0 copy-start.5
  0.7 0.0 copy-start.6
  0.7 0.0 copy-start.8
  0.7 0.0 copy-start
  0.7 0.0 copy-start.2
  0.8 0.6 %copy-done.9 = s32[256,4]{0,1:T(4,128)S(1)} copy-done((s32[256,4]{0,1:T(4,128)S(1)}, s32[256,4]{0,1:T(4,128)}, u32[]{:S(2)}) %copy-start.9) | copy-done | bytes 4120
  1.3 0.0 copy-done.10
  1.3 0.4 %copy-done.1 = f32[64,10,256]{2,0,1:T(8,128)S(1)} copy-done((f32[64,10,256]{2,0,1:T(8,128)S(1)}, f32[64,10,256]{2,0,1:T(8,128)}, u32[]{:S(2)}) %copy-start.1) | copy-done | bytes 655384
  1.8 0.0 copy-done.7
  1.8 0.1 copy-done.5
  1.8 3.3 %restrict.1 = f32[16,56,128]{2,1,0:T(8,128)} custom-call(bf16[128,256]{1,0:T(8,128)(2,1)S(1)} %constants.1.after_ref.counter_ref, f32[5,35,256]{2,1,0:T(8,128)S(1)} %bitcast.12, f32[35,64]{1,0:T(8,128)S(1)} %bitcast.14, f32[10,64,256]{2,1,0:T(8,128)S(1)} %bitcast.8, s32[4,256]{1,0:T(4,128)S(1)} %bitcast.15, s32[4,256]{1,0:T(4,128)S(1)} %bitcast.16), custom_call_target="tpu_custom_call" | custom-call | tf_op jit(solution)/shard_map/restrict/pallas_call | solution.py:34
  5.1 4.8 %all-to-all-start = ((f32[16,56,128]{2,1,0:T(8,128)}), f32[16,56,128]{2,1,0:T(8,128)S(1)}, u32[]{:S(2)}, u32[]{:S(2)}) async-start(f32[16,56,128]{2,1,0:T(8,128)} %restrict.1), calls=%async_computation | async-start | bytes 917504 | tf_op jit(solution)/shard_map/all_to_all | solution.py:507
  9.9 0.0 copy-done.6
  9.9 0.0 copy-done.8
  10.0 0.7 %prepare.1 = (bf16[256,512]{1,0:T(8,128)(2,1)S(1)}, bf16[50,960]{1,0:T(8,128)(2,1)S(1)}) custom-call(bf16[128,256]{1,0:T(8,128)(2,1)S(1)} %constants.1.after_ref.counter_ref, s32[4,128]{1,0:T(4,128)S(1)} %copy-done.8, f32[10,4,10]{2,1,0:T(4,128)S(1)} %bitcast.13), custom_call_target="tpu_custom_call" | custom-call | tf_op jit(solution)/shard_map/prepare/pallas_call | solution.py:34
  10.7 0.7 %copy-done.3 = bf16[256,512]{1,0:T(8,128)(2,1)} copy-done((bf16[256,512]{1,0:T(8,128)(2,1)}, bf16[256,512]{1,0:T(8,128)(2,1)S(1)}, u32[]{:S(2)}) %copy-start.3) | copy-done | bytes 262168
  11.4 0.0 copy-done
  11.4 0.0 copy-done.2
  11.4 0.4 pack_inner.1.after_ref
  11.7 0.0 copy-start.11
  11.7 0.4 pack_outer.1
  12.1 4.3 %collective-permute-start.1 = (f32[680,128]{1,0:T(8,128)S(1)}, f32[680,128]{1,0:T(8,128)S(1)}, u32[]{:S(2)}, u32[]{:S(2)}) collective-permute-start(f32[680,128]{1,0:T(8,128)S(1)} %pack_outer.1), channel_id=1, source_target_pairs={{1,2},{3,4},{5,6},{7,8},{9,10},{11,12},{13,14},{15,16},{17,18},{19... | collective-permute-start | bytes 1044488 | tf_op jit(solution)/shard_map/ppermute | solution.py:555
  16.4 0.1 collective-permute-start
  16.4 2.1 %all-to-all-done.columns_ref = f32[16,56,128]{2,1,0:T(8,128)S(1)} async-done(((f32[16,56,128]{2,1,0:T(8,128)}), f32[16,56,128]{2,1,0:T(8,128)S(1)}, u32[]{:S(2)}, u32[]{:S(2)}) %all-to-all-start) | async-done | bytes 458784 | tf_op jit(solution)/shard_map/all_to_all | solution.py:507
  18.6 0.4 seat_far.1
  18.9 0.4 %collective-permute-start.2 = (f32[50,128]{1,0:T(8,128)S(1)}, f32[50,128]{1,0:T(8,128)S(1)}, u32[]{:S(2)}, u32[]{:S(2)}) collective-permute-start(f32[50,128]{1,0:T(8,128)S(1)} %seat_far.1), channel_id=1, source_target_pairs={{0,16},{16,0},{1,17},{17,1},{2,18},{18,2},{3,19},{19,3},{4,20},{20... | collective-permute-start | bytes 76808 | tf_op jit(solution)/shard_map/ppermute | solution.py:50
  19.3 0.4 seat_near.1.refs_0_
  19.7 4.1 %collective-permute-done.2.refs_1_ = f32[50,128]{1,0:T(8,128)S(1)} collective-permute-done((f32[50,128]{1,0:T(8,128)S(1)}, f32[50,128]{1,0:T(8,128)S(1)}, u32[]{:S(2)}, u32[]{:S(2)}) %collective-permute-start.2) | collective-permute-done | bytes 25632 | tf_op jit(solution)/shard_map/ppermute | solution.py:50
  23.8 0.1 renumber.1.refs_0_
  23.9 0.0 collective-permute-start.5
  24.0 2.0 %collective-permute-start.4 = (f32[51,128]{1,0:T(8,128)S(1)}, f32[51,128]{1,0:T(8,128)S(1)}, u32[]{:S(2)}, u32[]{:S(2)}) collective-permute-start(f32[51,128]{1,0:T(8,128)S(1)} %renumber.1.refs_0_), channel_id=1, source_target_pairs={{0,2},{1,3},{2,0},{3,1},{4,6},{5,7},{6,4},{7,5},{8,10},{9,11},{10,... | collective-permute-start | bytes 78344 | tf_op jit(solution)/shard_map/ppermute | solution.py:50
  25.9 0.1 collective-permute-start.3
  26.0 0.0 collective-permute-done.5.refs_3_
  26.0 1.9 %collective-permute-done.4.refs_2_ = f32[51,128]{1,0:T(8,128)S(1)} collective-permute-done((f32[51,128]{1,0:T(8,128)S(1)}, f32[51,128]{1,0:T(8,128)S(1)}, u32[]{:S(2)}, u32[]{:S(2)}) %collective-permute-start.4) | collective-permute-done | bytes 26144 | tf_op jit(solution)/shard_map/ppermute | solution.py:50
  27.9 1.3 %collective-permute-done.3.refs_1_ = f32[51,128]{1,0:T(8,128)S(1)} collective-permute-done((f32[51,128]{1,0:T(8,128)S(1)}, f32[51,128]{1,0:T(8,128)S(1)}, u32[]{:S(2)}, u32[]{:S(2)}) %collective-permute-start.3) | collective-permute-done | bytes 26144 | tf_op jit(solution)/shard_map/ppermute | solution.py:50
  29.2 0.1 first.1
  29.4 1.9 %collective-permute-start.6 = (f32[32,128]{1,0:T(8,128)S(1)}, f32[32,128]{1,0:T(8,128)S(1)}, u32[]{:S(2)}, u32[]{:S(2)}) collective-permute-start(f32[32,128]{1,0:T(8,128)S(1)} %get-tuple-element.15), channel_id=1, source_target_pairs={{1,2},{3,4},{5,6},{7,8},{9,10},{11,12},{13,14},{15,16},{17,18},{19... | collective-permute-start | bytes 49160 | tf_op jit(solution)/shard_map/ppermute | solution.py:569
  31.3 0.8 %collective-permute-start.7 = (f32[32,128]{1,0:T(8,128)S(1)}, f32[32,128]{1,0:T(8,128)S(1)}, u32[]{:S(2)}, u32[]{:S(2)}) collective-permute-start(f32[32,128]{1,0:T(8,128)S(1)} %get-tuple-element.16), channel_id=1, source_target_pairs={{0,1},{1,0},{2,3},{3,2},{4,5},{5,4},{6,7},{7,6},{8,9},{9,8},{10,11... | collective-permute-start | bytes 49160 | tf_op jit(solution)/shard_map/ppermute | solution.py:570
  32.1 0.0 collective-permute-done.1.outer_ref
  32.1 0.0 collective-permute-done.inner_ref
  32.1 0.4 %beside.1 = (f32[50,50,128]{2,1,0:T(8,128)S(1)}, f32[100,128]{1,0:T(8,128)S(1)}, bf16[256,512]{1,0:T(8,128)(2,1)S(1)}) custom-call(f32[680,128]{1,0:T(8,128)S(1)} %collective-permute-done.inner_ref, f32[680,128]{1,0:T(8,128)S(1)} %collective-permute-done.1.outer_ref), custom_call_target="tpu_custom_call" | custom-call | tf_op jit(solution)/shard_map/beside/pallas_call | solution.py:34
  32.6 3.6 %collective-permute-done.6.outer_ref = f32[32,128]{1,0:T(8,128)S(1)} collective-permute-done((f32[32,128]{1,0:T(8,128)S(1)}, f32[32,128]{1,0:T(8,128)S(1)}, u32[]{:S(2)}, u32[]{:S(2)}) %collective-permute-start.6) | collective-permute-done | bytes 16416 | tf_op jit(solution)/shard_map/ppermute | solution.py:569
  36.2 0.0 collective-permute-done.7.inner_ref
  36.2 2.2 %sweeps.1 = (f32[50,128]{1,0:T(8,128)}, f32[50,128]{1,0:T(8,128)}) custom-call(f32[50,50,128]{2,1,0:T(8,128)S(1)} %copy-done, f32[50,50,128]{2,1,0:T(8,128)S(1)} %get-tuple-element.12.inverse_beside_ref, f32[50,128]{1,0:T(8,128)S(1)} %get-tuple-element.13.residual_ref, f32[64,128]{1,0:T(8,128)S(1)} %get-tuple-element.14.x_ref, ...), custom_call_target="tpu_custom_call" | custom-call | tf_op jit(solution)/shard_map/sweeps/pallas_call | solution.py:34
  (5 shorter events, 0.0 us)
Async XLA Ops:
  0.6 0.7 %copy-start.9 = (s32[256,4]{0,1:T(4,128)S(1)}, s32[256,4]{0,1:T(4,128)}, u32[]{:S(2)}) copy-start(s32[256,4]{0,1:T(4,128)} %param.14) | copy-start | bytes 12292
  0.6 0.7 %copy-start.10 = (s32[256,4]{0,1:T(4,128)S(1)}, s32[256,4]{0,1:T(4,128)}, u32[]{:S(2)}) copy-start(s32[256,4]{0,1:T(4,128)} %param.13) | copy-start | bytes 12292
  0.7 1.1 %copy-start.1 = (f32[64,10,256]{2,0,1:T(8,128)S(1)}, f32[64,10,256]{2,0,1:T(8,128)}, u32[]{:S(2)}) copy-start(f32[64,10,256]{2,0,1:T(8,128)} %param.12) | copy-start | bytes 1966084
  0.7 1.1 %copy-start.7 = (f32[64,35]{0,1:T(8,128)S(1)}, f32[64,35]{0,1:T(8,128)}, u32[]{:S(2)}) copy-start(f32[64,35]{0,1:T(8,128)} %param.11) | copy-start | bytes 26884
  0.7 1.1 %copy-start.5 = (f32[35,5,256]{2,0,1:T(8,128)S(1)}, f32[35,5,256]{2,0,1:T(8,128)}, u32[]{:S(2)}) copy-start(f32[35,5,256]{2,0,1:T(8,128)} %param.10) | copy-start | bytes 537604
  0.7 9.2 %copy-start.6 = (f32[4,10,10]{2,0,1:T(4,128)S(1)}, f32[4,10,10]{2,0,1:T(4,128)}, u32[]{:S(2)}) copy-start(f32[4,10,10]{2,0,1:T(4,128)} %param.18) | copy-start | bytes 4804
  0.7 9.2 %copy-start.8 = (s32[4,128]{1,0:T(4,128)S(1)}, s32[4,128]{1,0:T(4,128)}, u32[]{:S(2)}) copy-start(s32[4,128]{1,0:T(4,128)} %offset_ref.5) | copy-start | bytes 6148
  0.7 10.6 %copy-start = (f32[50,50,128]{2,1,0:T(8,128)S(1)}, f32[50,50,128]{2,1,0:T(8,128)}, u32[]{:S(2)}) copy-start(f32[50,50,128]{2,1,0:T(8,128)} %inverse_ref.7) | copy-start | bytes 3840004
  0.7 10.6 %copy-start.2 = (f32[4,5,5,128]{3,0,2,1:T(4,128)S(1)}, f32[4,5,5,128]{3,0,2,1:T(4,128)}, u32[]{:S(2)}) copy-start(f32[4,5,5,128]{3,0,2,1:T(4,128)} %param.17) | copy-start | bytes 153604
  5.1 13.5 %all-to-all-start = ((f32[16,56,128]{2,1,0:T(8,128)}), f32[16,56,128]{2,1,0:T(8,128)S(1)}, u32[]{:S(2)}, u32[]{:S(2)}) async-start(f32[16,56,128]{2,1,0:T(8,128)} %restrict.1), calls=%async_computation | async-start | bytes 917504 | tf_op jit(solution)/shard_map/all_to_all | solution.py:507
  10.7 0.7 %copy-start.3 = (bf16[256,512]{1,0:T(8,128)(2,1)}, bf16[256,512]{1,0:T(8,128)(2,1)S(1)}, u32[]{:S(2)}) copy-start(bf16[256,512]{1,0:T(8,128)(2,1)S(1)} %get-tuple-element.17.chooser_ref) | copy-start | bytes 786436
  11.7 12.1 %copy-start.11 = (s32[128]{0:T(128)S(1)}, s32[128]{0:T(128)}, u32[]{:S(2)}) copy-start(s32[128]{0:T(128)} %param.15) | copy-start | bytes 1540
  12.1 20.0 %collective-permute-start.1 = (f32[680,128]{1,0:T(8,128)S(1)}, f32[680,128]{1,0:T(8,128)S(1)}, u32[]{:S(2)}, u32[]{:S(2)}) collective-permute-start(f32[680,128]{1,0:T(8,128)S(1)} %pack_outer.1), channel_id=1, source_target_pairs={{1,2},{3,4},{5,6},{7,8},{9,10},{11,12},{13,14},{15,16},{17,18},{19... | collective-permute-start | bytes 1044488 | tf_op jit(solution)/shard_map/ppermute | solution.py:555
  16.4 15.8 %collective-permute-start = (f32[680,128]{1,0:T(8,128)S(1)}, f32[680,128]{1,0:T(8,128)S(1)}, u32[]{:S(2)}, u32[]{:S(2)}) collective-permute-start(f32[680,128]{1,0:T(8,128)S(1)} %pack_inner.1.after_ref), channel_id=1, source_target_pairs={{0,1},{1,0},{2,3},{3,2},{4,5},{5,4},{6,7},{7,6},{8,9},{9,8},{10,11... | collective-permute-start | bytes 1044488 | tf_op jit(solution)/shard_map/ppermute | solution.py:554
  18.9 17.3 %copy-start.4 = (bf16[256,512]{1,0:T(8,128)(2,1)S(1)}, bf16[256,512]{1,0:T(8,128)(2,1)}, u32[]{:S(2)}) copy-start(bf16[256,512]{1,0:T(8,128)(2,1)} %copy-done.3) | copy-start | bytes 786436
  18.9 4.8 %collective-permute-start.2 = (f32[50,128]{1,0:T(8,128)S(1)}, f32[50,128]{1,0:T(8,128)S(1)}, u32[]{:S(2)}, u32[]{:S(2)}) collective-permute-start(f32[50,128]{1,0:T(8,128)S(1)} %seat_far.1), channel_id=1, source_target_pairs={{0,16},{16,0},{1,17},{17,1},{2,18},{18,2},{3,19},{19,3},{4,20},{20... | collective-permute-start | bytes 76808 | tf_op jit(solution)/shard_map/ppermute | solution.py:50
  23.9 2.1 %collective-permute-start.5 = (f32[51,128]{1,0:T(8,128)S(1)}, f32[51,128]{1,0:T(8,128)S(1)}, u32[]{:S(2)}, u32[]{:S(2)}) collective-permute-start(f32[51,128]{1,0:T(8,128)S(1)} %renumber.1.refs_0_), channel_id=1, source_target_pairs={{0,1},{1,0},{2,3},{3,2},{4,5},{5,4},{6,7},{7,6},{8,9},{9,8},{10,11... | collective-permute-start | bytes 78344 | tf_op jit(solution)/shard_map/ppermute | solution.py:50
  24.0 3.9 %collective-permute-start.4 = (f32[51,128]{1,0:T(8,128)S(1)}, f32[51,128]{1,0:T(8,128)S(1)}, u32[]{:S(2)}, u32[]{:S(2)}) collective-permute-start(f32[51,128]{1,0:T(8,128)S(1)} %renumber.1.refs_0_), channel_id=1, source_target_pairs={{0,2},{1,3},{2,0},{3,1},{4,6},{5,7},{6,4},{7,5},{8,10},{9,11},{10,... | collective-permute-start | bytes 78344 | tf_op jit(solution)/shard_map/ppermute | solution.py:50
  25.9 3.3 %collective-permute-start.3 = (f32[51,128]{1,0:T(8,128)S(1)}, f32[51,128]{1,0:T(8,128)S(1)}, u32[]{:S(2)}, u32[]{:S(2)}) collective-permute-start(f32[51,128]{1,0:T(8,128)S(1)} %renumber.1.refs_0_), channel_id=1, source_target_pairs={{0,3},{1,2},{2,1},{3,0},{4,7},{5,6},{6,5},{7,4},{8,11},{9,10},{10,... | collective-permute-start | bytes 78344 | tf_op jit(solution)/shard_map/ppermute | solution.py:50
  29.4 6.9 %collective-permute-start.6 = (f32[32,128]{1,0:T(8,128)S(1)}, f32[32,128]{1,0:T(8,128)S(1)}, u32[]{:S(2)}, u32[]{:S(2)}) collective-permute-start(f32[32,128]{1,0:T(8,128)S(1)} %get-tuple-element.15), channel_id=1, source_target_pairs={{1,2},{3,4},{5,6},{7,8},{9,10},{11,12},{13,14},{15,16},{17,18},{19... | collective-permute-start | bytes 49160 | tf_op jit(solution)/shard_map/ppermute | solution.py:569
  31.3 4.9 %collective-permute-start.7 = (f32[32,128]{1,0:T(8,128)S(1)}, f32[32,128]{1,0:T(8,128)S(1)}, u32[]{:S(2)}, u32[]{:S(2)}) collective-permute-start(f32[32,128]{1,0:T(8,128)S(1)} %get-tuple-element.16), channel_id=1, source_target_pairs={{0,1},{1,0},{2,3},{3,2},{4,5},{5,4},{6,7},{7,6},{8,9},{9,8},{10,11... | collective-permute-start | bytes 49160 | tf_op jit(solution)/shard_map/ppermute | solution.py:570

commit v2 on v1

--- a/solution.py
+++ b/solution.py
@@ -547,7 +547,7 @@
                 functools.partial(pack_kernel, outer=outer),
                 "pack_outer" if outer else "pack_inner",
                 packed,
-                (packs[0] if outer else lift, block_inverse, jacobian, face_offset),
+                (packs[0] if outer else counter, block_inverse, jacobian, face_offset),
                 [pltpu.VMEM((lines, block), F32)],
             )
         )

time: 38.7 us -> 38.6 us (level)
  starting transfers between devices: 14.4 us -> 15.2 us
  local copies, waits for them, and re-layouts: 1.81 us -> 1.16 us
  waiting for transfers between devices: 13.1 us -> 12.7 us
    all_to_all x1, waiting for transfers between devices: 2.12 us -> 4.35 us  [per_device(): columns = lax.all_to_all(columns, PLANE, 0, 0, tiled=True)]
    ppermute x1, waiting for transfers between devices: 3.65 us -> 1.82 us  [per_device(): outer = lax.ppermute(to_outer, WHOLE, outer_pairs)]
    ppermute x1, starting transfers between devices: 0.84 us -> 1.95 us  [per_device(): inner = lax.ppermute(to_inner, WHOLE, inner_pairs)]
    ppermute x4, waiting for transfers between devices: 7.28 us -> 6.51 us  [swap_all(): lax.ppermute(blocks[d], axis, [(i, i ^ d) for i in range(count)])]
    unnamed x24 -> x20, local copies, waits for them, and re-layouts: 1.81 us -> 1.16 us
where the time goes in v2:
time: 38.6 us; the launch traced here: 38.3 us
  starting transfers between devices  15.2 us (39%)
  waiting for transfers between devices  12.7 us (33%)
  Pallas kernels  8.32 us (22%)
  local copies, waits for them, and re-layouts  1.16 us (3%)
  between operations  0.85 us (2%)
    pallas_call x11, Pallas kernels, call(): pl.pallas_call(kernel, out_shape=out, in_specs=[VMEM] * len(args), out_sp...  8.32 us
    ppermute x4, waiting for transfers between devices, swap_all(): lax.ppermute(blocks[d], axis, [(i, i ^ d) for i in range(count)])  6.51 us
    all_to_all x1, starting transfers between devices, per_device(): columns = lax.all_to_all(columns, PLANE, 0, 0, tiled=True)  4.85 us
    all_to_all x1, waiting for transfers between devices, per_device(): columns = lax.all_to_all(columns, PLANE, 0, 0, tiled=True)  4.35 us
    ppermute x1, starting transfers between devices, per_device(): outer = lax.ppermute(packs[1], WHOLE, outer_pairs)  4.26 us
    ppermute x4, starting transfers between devices, swap_all(): lax.ppermute(blocks[d], axis, [(i, i ^ d) for i in range(count)])  2.19 us
    ppermute x1, starting transfers between devices, per_device(): inner = lax.ppermute(to_inner, WHOLE, inner_pairs)  1.95 us
    ppermute x1, starting transfers between devices, per_device(): outer = lax.ppermute(to_outer, WHOLE, outer_pairs)  1.92 us
  transfers between devices with their start and end apart: 9, of which 5 were waited for; matrix products, arithmetic and copies ran while one was open for 0% of the time, Pallas kernels for 7%

profile of v2, /device:TPU:16, one launch (start us, length us, event | category | flops | bytes accessed | tf_op | source)
XLA Modules:
  0.0 38.3 jit_solution(18157567002595278637)
XLA Ops:
  0.6 0.0 copy-start.3
  0.6 0.0 copy-start.5
  0.7 0.0 copy-start.1
  0.7 0.0 copy-start.7
  0.7 0.0 copy-start.8
  0.7 0.0 copy-start
  0.7 0.0 copy-start.2
  0.7 0.0 copy-start.6
  0.7 0.8 %copy-done.3 = f32[35,5,256]{2,0,1:T(8,128)S(1)} copy-done((f32[35,5,256]{2,0,1:T(8,128)S(1)}, f32[35,5,256]{2,0,1:T(8,128)}, u32[]{:S(2)}) %copy-start.3) | copy-done | bytes 179224
  1.6 0.0 copy-done.5
  1.6 0.3 copy-done.1
  1.9 0.0 copy-done.7
  1.9 0.0 copy-done.8
  1.9 3.3 %restrict.1 = f32[16,56,128]{2,1,0:T(8,128)} custom-call(bf16[128,256]{1,0:T(8,128)(2,1)S(1)} %constants.1.after_ref.counter_ref, f32[5,35,256]{2,1,0:T(8,128)S(1)} %bitcast.12, f32[35,64]{1,0:T(8,128)S(1)} %bitcast.14, f32[10,64,256]{2,1,0:T(8,128)S(1)} %bitcast.8, s32[4,256]{1,0:T(4,128)S(1)} %bitcast.15, s32[4,256]{1,0:T(4,128)S(1)} %bitcast.16), custom_call_target="tpu_custom_call" | custom-call | tf_op jit(solution)/shard_map/restrict/pallas_call | solution.py:34
  5.1 4.9 %all-to-all-start = ((f32[16,56,128]{2,1,0:T(8,128)}), f32[16,56,128]{2,1,0:T(8,128)S(1)}, u32[]{:S(2)}, u32[]{:S(2)}) async-start(f32[16,56,128]{2,1,0:T(8,128)} %restrict.1), calls=%async_computation | async-start | bytes 917504 | tf_op jit(solution)/shard_map/all_to_all | solution.py:507
  10.0 0.0 copy-done
  10.0 0.0 copy-done.2
  10.0 0.0 copy-done.6
  10.0 0.4 pack_inner.1.after_ref
  10.4 0.0 copy-start.9
  10.4 0.4 pack_outer.1
  10.8 0.0 copy-start.4
  10.8 4.3 %collective-permute-start.1 = (f32[680,128]{1,0:T(8,128)S(1)}, f32[680,128]{1,0:T(8,128)S(1)}, u32[]{:S(2)}, u32[]{:S(2)}) collective-permute-start(f32[680,128]{1,0:T(8,128)S(1)} %pack_outer.1), channel_id=1, source_target_pairs={{1,2},{3,4},{5,6},{7,8},{9,10},{11,12},{13,14},{15,16},{17,18},{19... | collective-permute-start | bytes 1044488 | tf_op jit(solution)/shard_map/ppermute | solution.py:555
  15.0 0.1 collective-permute-start
  15.1 4.4 %all-to-all-done.columns_ref = f32[16,56,128]{2,1,0:T(8,128)S(1)} async-done(((f32[16,56,128]{2,1,0:T(8,128)}), f32[16,56,128]{2,1,0:T(8,128)S(1)}, u32[]{:S(2)}, u32[]{:S(2)}) %all-to-all-start) | async-done | bytes 458784 | tf_op jit(solution)/shard_map/all_to_all | solution.py:507
  19.5 0.4 seat_far.1
  19.8 0.1 collective-permute-start.2
  19.9 0.4 seat_near.1.refs_0_
  20.3 4.5 %collective-permute-done.2.refs_1_ = f32[50,128]{1,0:T(8,128)S(1)} collective-permute-done((f32[50,128]{1,0:T(8,128)S(1)}, f32[50,128]{1,0:T(8,128)S(1)}, u32[]{:S(2)}, u32[]{:S(2)}) %collective-permute-start.2) | collective-permute-done | bytes 25632 | tf_op jit(solution)/shard_map/ppermute | solution.py:50
  24.8 0.0 copy-done.9
  24.8 0.1 renumber.1.refs_0_
  24.9 0.0 collective-permute-start.3
  24.9 2.0 %collective-permute-start.4 = (f32[51,128]{1,0:T(8,128)S(1)}, f32[51,128]{1,0:T(8,128)S(1)}, u32[]{:S(2)}, u32[]{:S(2)}) collective-permute-start(f32[51,128]{1,0:T(8,128)S(1)} %renumber.1.refs_0_), channel_id=1, source_target_pairs={{0,2},{1,3},{2,0},{3,1},{4,6},{5,7},{6,4},{7,5},{8,10},{9,11},{10,... | collective-permute-start | bytes 78344 | tf_op jit(solution)/shard_map/ppermute | solution.py:50
  27.0 0.0 collective-permute-start.5
  27.0 1.2 %collective-permute-done.3.refs_1_ = f32[51,128]{1,0:T(8,128)S(1)} collective-permute-done((f32[51,128]{1,0:T(8,128)S(1)}, f32[51,128]{1,0:T(8,128)S(1)}, u32[]{:S(2)}, u32[]{:S(2)}) %collective-permute-start.3) | collective-permute-done | bytes 26144 | tf_op jit(solution)/shard_map/ppermute | solution.py:50
  28.2 0.8 %collective-permute-done.4.refs_2_ = f32[51,128]{1,0:T(8,128)S(1)} collective-permute-done((f32[51,128]{1,0:T(8,128)S(1)}, f32[51,128]{1,0:T(8,128)S(1)}, u32[]{:S(2)}, u32[]{:S(2)}) %collective-permute-start.4) | collective-permute-done | bytes 26144 | tf_op jit(solution)/shard_map/ppermute | solution.py:50
  29.1 0.0 collective-permute-done.5.refs_3_
  29.1 0.1 first.1
  29.2 1.9 %collective-permute-start.6 = (f32[32,128]{1,0:T(8,128)S(1)}, f32[32,128]{1,0:T(8,128)S(1)}, u32[]{:S(2)}, u32[]{:S(2)}) collective-permute-start(f32[32,128]{1,0:T(8,128)S(1)} %get-tuple-element.14), channel_id=1, source_target_pairs={{1,2},{3,4},{5,6},{7,8},{9,10},{11,12},{13,14},{15,16},{17,18},{19... | collective-permute-start | bytes 49160 | tf_op jit(solution)/shard_map/ppermute | solution.py:569
  31.2 2.0 %collective-permute-start.7 = (f32[32,128]{1,0:T(8,128)S(1)}, f32[32,128]{1,0:T(8,128)S(1)}, u32[]{:S(2)}, u32[]{:S(2)}) collective-permute-start(f32[32,128]{1,0:T(8,128)S(1)} %get-tuple-element.15), channel_id=1, source_target_pairs={{0,1},{1,0},{2,3},{3,2},{4,5},{5,4},{6,7},{7,6},{8,9},{9,8},{10,11... | collective-permute-start | bytes 49160 | tf_op jit(solution)/shard_map/ppermute | solution.py:570
  33.1 0.0 copy-done.4
  33.1 0.7 %prepare.1 = (bf16[256,512]{1,0:T(8,128)(2,1)S(1)}, bf16[50,960]{1,0:T(8,128)(2,1)S(1)}) custom-call(bf16[128,256]{1,0:T(8,128)(2,1)S(1)} %constants.1.after_ref.counter_ref, s32[4,128]{1,0:T(4,128)S(1)} %copy-done.6, f32[10,4,10]{2,1,0:T(4,128)S(1)} %bitcast.13), custom_call_target="tpu_custom_call" | custom-call | tf_op jit(solution)/shard_map/prepare/pallas_call | solution.py:34
  33.8 0.0 collective-permute-done.1.outer_ref
  33.8 0.0 collective-permute-done.inner_ref
  33.8 0.4 %beside.1 = (f32[50,50,128]{2,1,0:T(8,128)S(1)}, f32[100,128]{1,0:T(8,128)S(1)}, bf16[256,512]{1,0:T(8,128)(2,1)S(1)}) custom-call(f32[680,128]{1,0:T(8,128)S(1)} %collective-permute-done.inner_ref, f32[680,128]{1,0:T(8,128)S(1)} %collective-permute-done.1.outer_ref), custom_call_target="tpu_custom_call" | custom-call | tf_op jit(solution)/shard_map/beside/pallas_call | solution.py:34
  34.3 1.8 %collective-permute-done.6.outer_ref = f32[32,128]{1,0:T(8,128)S(1)} collective-permute-done((f32[32,128]{1,0:T(8,128)S(1)}, f32[32,128]{1,0:T(8,128)S(1)}, u32[]{:S(2)}, u32[]{:S(2)}) %collective-permute-start.6) | collective-permute-done | bytes 16416 | tf_op jit(solution)/shard_map/ppermute | solution.py:569
  36.1 0.0 collective-permute-done.7.inner_ref
  36.1 2.2 %sweeps.1 = (f32[50,128]{1,0:T(8,128)}, f32[50,128]{1,0:T(8,128)}) custom-call(f32[50,50,128]{2,1,0:T(8,128)S(1)} %copy-done, f32[50,50,128]{2,1,0:T(8,128)S(1)} %get-tuple-element.11.inverse_beside_ref, f32[50,128]{1,0:T(8,128)S(1)} %get-tuple-element.12.residual_ref, f32[64,128]{1,0:T(8,128)S(1)} %get-tuple-element.13.x_ref, ...), custom_call_target="tpu_custom_call" | custom-call | tf_op jit(solution)/shard_map/sweeps/pallas_call | solution.py:34
  (1 shorter events, 0.0 us)
Async XLA Ops:
  0.6 0.9 %copy-start.3 = (f32[35,5,256]{2,0,1:T(8,128)S(1)}, f32[35,5,256]{2,0,1:T(8,128)}, u32[]{:S(2)}) copy-start(f32[35,5,256]{2,0,1:T(8,128)} %param.10) | copy-start | bytes 537604
  0.6 0.9 %copy-start.5 = (f32[64,35]{0,1:T(8,128)S(1)}, f32[64,35]{0,1:T(8,128)}, u32[]{:S(2)}) copy-start(f32[64,35]{0,1:T(8,128)} %param.11) | copy-start | bytes 26884
  0.7 1.2 %copy-start.1 = (f32[64,10,256]{2,0,1:T(8,128)S(1)}, f32[64,10,256]{2,0,1:T(8,128)}, u32[]{:S(2)}) copy-start(f32[64,10,256]{2,0,1:T(8,128)} %param.12) | copy-start | bytes 1966084
  0.7 1.2 %copy-start.7 = (s32[256,4]{0,1:T(4,128)S(1)}, s32[256,4]{0,1:T(4,128)}, u32[]{:S(2)}) copy-start(s32[256,4]{0,1:T(4,128)} %param.14) | copy-start | bytes 12292
  0.7 1.2 %copy-start.8 = (s32[256,4]{0,1:T(4,128)S(1)}, s32[256,4]{0,1:T(4,128)}, u32[]{:S(2)}) copy-start(s32[256,4]{0,1:T(4,128)} %param.13) | copy-start | bytes 12292
  0.7 9.3 %copy-start = (f32[50,50,128]{2,1,0:T(8,128)S(1)}, f32[50,50,128]{2,1,0:T(8,128)}, u32[]{:S(2)}) copy-start(f32[50,50,128]{2,1,0:T(8,128)} %inverse_ref.7) | copy-start | bytes 3840004
  0.7 9.3 %copy-start.2 = (f32[4,5,5,128]{3,0,2,1:T(4,128)S(1)}, f32[4,5,5,128]{3,0,2,1:T(4,128)}, u32[]{:S(2)}) copy-start(f32[4,5,5,128]{3,0,2,1:T(4,128)} %param.17) | copy-start | bytes 153604
  0.7 9.3 %copy-start.6 = (s32[4,128]{1,0:T(4,128)S(1)}, s32[4,128]{1,0:T(4,128)}, u32[]{:S(2)}) copy-start(s32[4,128]{1,0:T(4,128)} %offset_ref.5) | copy-start | bytes 6148
  5.1 14.3 %all-to-all-start = ((f32[16,56,128]{2,1,0:T(8,128)}), f32[16,56,128]{2,1,0:T(8,128)S(1)}, u32[]{:S(2)}, u32[]{:S(2)}) async-start(f32[16,56,128]{2,1,0:T(8,128)} %restrict.1), calls=%async_computation | async-start | bytes 917504 | tf_op jit(solution)/shard_map/all_to_all | solution.py:507
  10.4 14.4 %copy-start.9 = (s32[128]{0:T(128)S(1)}, s32[128]{0:T(128)}, u32[]{:S(2)}) copy-start(s32[128]{0:T(128)} %param.15) | copy-start | bytes 1540
  10.8 22.4 %copy-start.4 = (f32[4,10,10]{2,0,1:T(4,128)S(1)}, f32[4,10,10]{2,0,1:T(4,128)}, u32[]{:S(2)}) copy-start(f32[4,10,10]{2,0,1:T(4,128)} %param.18) | copy-start | bytes 4804
  10.8 23.0 %collective-permute-start.1 = (f32[680,128]{1,0:T(8,128)S(1)}, f32[680,128]{1,0:T(8,128)S(1)}, u32[]{:S(2)}, u32[]{:S(2)}) collective-permute-start(f32[680,128]{1,0:T(8,128)S(1)} %pack_outer.1), channel_id=1, source_target_pairs={{1,2},{3,4},{5,6},{7,8},{9,10},{11,12},{13,14},{15,16},{17,18},{19... | collective-permute-start | bytes 1044488 | tf_op jit(solution)/shard_map/ppermute | solution.py:555
  15.0 18.8 %collective-permute-start = (f32[680,128]{1,0:T(8,128)S(1)}, f32[680,128]{1,0:T(8,128)S(1)}, u32[]{:S(2)}, u32[]{:S(2)}) collective-permute-start(f32[680,128]{1,0:T(8,128)S(1)} %pack_inner.1.after_ref), channel_id=1, source_target_pairs={{0,1},{1,0},{2,3},{3,2},{4,5},{5,4},{6,7},{7,6},{8,9},{9,8},{10,11... | collective-permute-start | bytes 1044488 | tf_op jit(solution)/shard_map/ppermute | solution.py:554
  19.8 4.9 %collective-permute-start.2 = (f32[50,128]{1,0:T(8,128)S(1)}, f32[50,128]{1,0:T(8,128)S(1)}, u32[]{:S(2)}, u32[]{:S(2)}) collective-permute-start(f32[50,128]{1,0:T(8,128)S(1)} %seat_far.1), channel_id=1, source_target_pairs={{0,16},{16,0},{1,17},{17,1},{2,18},{18,2},{3,19},{19,3},{4,20},{20... | collective-permute-start | bytes 76808 | tf_op jit(solution)/shard_map/ppermute | solution.py:50
  24.9 3.3 %collective-permute-start.3 = (f32[51,128]{1,0:T(8,128)S(1)}, f32[51,128]{1,0:T(8,128)S(1)}, u32[]{:S(2)}, u32[]{:S(2)}) collective-permute-start(f32[51,128]{1,0:T(8,128)S(1)} %renumber.1.refs_0_), channel_id=1, source_target_pairs={{0,3},{1,2},{2,1},{3,0},{4,7},{5,6},{6,5},{7,4},{8,11},{9,10},{10,... | collective-permute-start | bytes 78344 | tf_op jit(solution)/shard_map/ppermute | solution.py:50
  24.9 4.1 %collective-permute-start.4 = (f32[51,128]{1,0:T(8,128)S(1)}, f32[51,128]{1,0:T(8,128)S(1)}, u32[]{:S(2)}, u32[]{:S(2)}) collective-permute-start(f32[51,128]{1,0:T(8,128)S(1)} %renumber.1.refs_0_), channel_id=1, source_target_pairs={{0,2},{1,3},{2,0},{3,1},{4,6},{5,7},{6,4},{7,5},{8,10},{9,11},{10,... | collective-permute-start | bytes 78344 | tf_op jit(solution)/shard_map/ppermute | solution.py:50
  27.0 2.1 %collective-permute-start.5 = (f32[51,128]{1,0:T(8,128)S(1)}, f32[51,128]{1,0:T(8,128)S(1)}, u32[]{:S(2)}, u32[]{:S(2)}) collective-permute-start(f32[51,128]{1,0:T(8,128)S(1)} %renumber.1.refs_0_), channel_id=1, source_target_pairs={{0,1},{1,0},{2,3},{3,2},{4,5},{5,4},{6,7},{7,6},{8,9},{9,8},{10,11... | collective-permute-start | bytes 78344 | tf_op jit(solution)/shard_map/ppermute | solution.py:50
  29.2 6.9 %collective-permute-start.6 = (f32[32,128]{1,0:T(8,128)S(1)}, f32[32,128]{1,0:T(8,128)S(1)}, u32[]{:S(2)}, u32[]{:S(2)}) collective-permute-start(f32[32,128]{1,0:T(8,128)S(1)} %get-tuple-element.14), channel_id=1, source_target_pairs={{1,2},{3,4},{5,6},{7,8},{9,10},{11,12},{13,14},{15,16},{17,18},{19... | collective-permute-start | bytes 49160 | tf_op jit(solution)/shard_map/ppermute | solution.py:569
  31.2 4.9 %collective-permute-start.7 = (f32[32,128]{1,0:T(8,128)S(1)}, f32[32,128]{1,0:T(8,128)S(1)}, u32[]{:S(2)}, u32[]{:S(2)}) collective-permute-start(f32[32,128]{1,0:T(8,128)S(1)} %get-tuple-element.15), channel_id=1, source_target_pairs={{0,1},{1,0},{2,3},{3,2},{4,5},{5,4},{6,7},{7,6},{8,9},{9,8},{10,11... | collective-permute-start | bytes 49160 | tf_op jit(solution)/shard_map/ppermute | solution.py:570

commit v3 on v2

--- a/solution.py
+++ b/solution.py
@@ -201,15 +201,17 @@
         j, at = divmod(group * capacity, columns_ref.shape[2])
         got = jnp.concatenate(
             [
-                columns_ref[s, j * rows : j * rows + full + 1, at : at + capacity]
+                columns_ref[s, j * rows : (j + 1) * rows, at : at + capacity]
                 for s in range(sources)
             ],
             axis=1,
         )
         seat = got[full : full + 1, :]
         chooser = (rows_of((block, got.shape[1]), 0).astype(F32) == seat).astype(F32).astype(BF16)
-        high, low = split(got)
-        dense = (mm(high, chooser, 1, 1) + mm(low, chooser, 1, 1))[:full]
+        high = got.astype(BF16).astype(F32)
+        both = jnp.concatenate([high, got - high], axis=0).astype(BF16)
+        dense = mm(both, chooser, 1, 1)
+        dense = (dense[:rows] + dense[rows:])[:full]
         if len(out_refs) == len(groups):
             out_refs[n][...] = dense
         else:

time: 38.6 us -> 38.5 us (level)
  no operation moved by 1% of the time
where the time goes in v3:
time: 38.5 us; the launch traced here: 38.2 us
  starting transfers between devices  15.2 us (39%)
  waiting for transfers between devices  12.8 us (33%)
  Pallas kernels  8.21 us (21%)
  local copies, waits for them, and re-layouts  1.16 us (3%)
  between operations  0.85 us (2%)
    pallas_call x11, Pallas kernels, call(): pl.pallas_call(kernel, out_shape=out, in_specs=[VMEM] * len(args), out_sp...  8.21 us
    ppermute x4, waiting for transfers between devices, swap_all(): lax.ppermute(blocks[d], axis, [(i, i ^ d) for i in range(count)])  6.57 us
    all_to_all x1, starting transfers between devices, per_device(): columns = lax.all_to_all(columns, PLANE, 0, 0, tiled=True)  4.85 us
    all_to_all x1, waiting for transfers between devices, per_device(): columns = lax.all_to_all(columns, PLANE, 0, 0, tiled=True)  4.35 us
    ppermute x1, starting transfers between devices, per_device(): outer = lax.ppermute(packs[1], WHOLE, outer_pairs)  4.26 us
    ppermute x4, starting transfers between devices, swap_all(): lax.ppermute(blocks[d], axis, [(i, i ^ d) for i in range(count)])  2.19 us
    ppermute x1, starting transfers between devices, per_device(): inner = lax.ppermute(to_inner, WHOLE, inner_pairs)  1.95 us
    ppermute x1, starting transfers between devices, per_device(): outer = lax.ppermute(to_outer, WHOLE, outer_pairs)  1.92 us
  transfers between devices with their start and end apart: 9, of which 5 were waited for; matrix products, arithmetic and copies ran while one was open for 0% of the time, Pallas kernels for 7%

profile of v3, /device:TPU:16, one launch (start us, length us, event | category | flops | bytes accessed | tf_op | source)
XLA Modules:
  0.0 38.2 jit_solution(13465434590274640184)
XLA Ops:
  0.6 0.0 copy-start.3
  0.6 0.0 copy-start.5
  0.7 0.0 copy-start.1
  0.7 0.0 copy-start.7
  0.7 0.0 copy-start.8
  0.7 0.0 copy-start
  0.7 0.0 copy-start.2
  0.7 0.0 copy-start.6
  0.7 0.8 %copy-done.3 = f32[35,5,256]{2,0,1:T(8,128)S(1)} copy-done((f32[35,5,256]{2,0,1:T(8,128)S(1)}, f32[35,5,256]{2,0,1:T(8,128)}, u32[]{:S(2)}) %copy-start.3) | copy-done | bytes 179224
  1.6 0.0 copy-done.5
  1.6 0.3 copy-done.1
  1.9 0.0 copy-done.7
  1.9 0.0 copy-done.8
  1.9 3.3 %restrict.1 = f32[16,56,128]{2,1,0:T(8,128)} custom-call(bf16[128,256]{1,0:T(8,128)(2,1)S(1)} %constants.1.after_ref.counter_ref, f32[5,35,256]{2,1,0:T(8,128)S(1)} %bitcast.12, f32[35,64]{1,0:T(8,128)S(1)} %bitcast.14, f32[10,64,256]{2,1,0:T(8,128)S(1)} %bitcast.8, s32[4,256]{1,0:T(4,128)S(1)} %bitcast.15, s32[4,256]{1,0:T(4,128)S(1)} %bitcast.16), custom_call_target="tpu_custom_call" | custom-call | tf_op jit(solution)/shard_map/restrict/pallas_call | solution.py:34
  5.1 4.9 %all-to-all-start = ((f32[16,56,128]{2,1,0:T(8,128)}), f32[16,56,128]{2,1,0:T(8,128)S(1)}, u32[]{:S(2)}, u32[]{:S(2)}) async-start(f32[16,56,128]{2,1,0:T(8,128)} %restrict.1), calls=%async_computation | async-start | bytes 917504 | tf_op jit(solution)/shard_map/all_to_all | solution.py:509
  10.0 0.0 copy-done
  10.0 0.0 copy-done.2
  10.0 0.0 copy-done.6
  10.0 0.4 pack_inner.1.after_ref
  10.4 0.0 copy-start.9
  10.4 0.4 pack_outer.1
  10.8 0.0 copy-start.4
  10.8 4.3 %collective-permute-start.1 = (f32[680,128]{1,0:T(8,128)S(1)}, f32[680,128]{1,0:T(8,128)S(1)}, u32[]{:S(2)}, u32[]{:S(2)}) collective-permute-start(f32[680,128]{1,0:T(8,128)S(1)} %pack_outer.1), channel_id=1, source_target_pairs={{1,2},{3,4},{5,6},{7,8},{9,10},{11,12},{13,14},{15,16},{17,18},{19... | collective-permute-start | bytes 1044488 | tf_op jit(solution)/shard_map/ppermute | solution.py:557
  15.0 0.1 collective-permute-start
  15.1 4.4 %all-to-all-done.columns_ref = f32[16,56,128]{2,1,0:T(8,128)S(1)} async-done(((f32[16,56,128]{2,1,0:T(8,128)}), f32[16,56,128]{2,1,0:T(8,128)S(1)}, u32[]{:S(2)}, u32[]{:S(2)}) %all-to-all-start) | async-done | bytes 458784 | tf_op jit(solution)/shard_map/all_to_all | solution.py:509
  19.5 0.3 seat_far.1
  19.8 0.1 collective-permute-start.2
  19.9 0.3 seat_near.1.refs_0_
  20.2 4.5 %collective-permute-done.2.refs_1_ = f32[50,128]{1,0:T(8,128)S(1)} collective-permute-done((f32[50,128]{1,0:T(8,128)S(1)}, f32[50,128]{1,0:T(8,128)S(1)}, u32[]{:S(2)}, u32[]{:S(2)}) %collective-permute-start.2) | collective-permute-done | bytes 25632 | tf_op jit(solution)/shard_map/ppermute | solution.py:50
  24.7 0.0 copy-done.9
  24.7 0.1 renumber.1.refs_0_
  24.8 0.0 collective-permute-start.3
  24.9 2.0 %collective-permute-start.4 = (f32[51,128]{1,0:T(8,128)S(1)}, f32[51,128]{1,0:T(8,128)S(1)}, u32[]{:S(2)}, u32[]{:S(2)}) collective-permute-start(f32[51,128]{1,0:T(8,128)S(1)} %renumber.1.refs_0_), channel_id=1, source_target_pairs={{0,2},{1,3},{2,0},{3,1},{4,6},{5,7},{6,4},{7,5},{8,10},{9,11},{10,... | collective-permute-start | bytes 78344 | tf_op jit(solution)/shard_map/ppermute | solution.py:50
  26.9 0.0 collective-permute-start.5
  27.0 1.2 %collective-permute-done.3.refs_1_ = f32[51,128]{1,0:T(8,128)S(1)} collective-permute-done((f32[51,128]{1,0:T(8,128)S(1)}, f32[51,128]{1,0:T(8,128)S(1)}, u32[]{:S(2)}, u32[]{:S(2)}) %collective-permute-start.3) | collective-permute-done | bytes 26144 | tf_op jit(solution)/shard_map/ppermute | solution.py:50
  28.2 0.8 %collective-permute-done.4.refs_2_ = f32[51,128]{1,0:T(8,128)S(1)} collective-permute-done((f32[51,128]{1,0:T(8,128)S(1)}, f32[51,128]{1,0:T(8,128)S(1)}, u32[]{:S(2)}, u32[]{:S(2)}) %collective-permute-start.4) | collective-permute-done | bytes 26144 | tf_op jit(solution)/shard_map/ppermute | solution.py:50
  29.0 0.0 collective-permute-done.5.refs_3_
  29.0 0.1 first.1
  29.2 1.9 %collective-permute-start.6 = (f32[32,128]{1,0:T(8,128)S(1)}, f32[32,128]{1,0:T(8,128)S(1)}, u32[]{:S(2)}, u32[]{:S(2)}) collective-permute-start(f32[32,128]{1,0:T(8,128)S(1)} %get-tuple-element.14), channel_id=1, source_target_pairs={{1,2},{3,4},{5,6},{7,8},{9,10},{11,12},{13,14},{15,16},{17,18},{19... | collective-permute-start | bytes 49160 | tf_op jit(solution)/shard_map/ppermute | solution.py:571
  31.1 2.0 %collective-permute-start.7 = (f32[32,128]{1,0:T(8,128)S(1)}, f32[32,128]{1,0:T(8,128)S(1)}, u32[]{:S(2)}, u32[]{:S(2)}) collective-permute-start(f32[32,128]{1,0:T(8,128)S(1)} %get-tuple-element.15), channel_id=1, source_target_pairs={{0,1},{1,0},{2,3},{3,2},{4,5},{5,4},{6,7},{7,6},{8,9},{9,8},{10,11... | collective-permute-start | bytes 49160 | tf_op jit(solution)/shard_map/ppermute | solution.py:572
  33.0 0.0 copy-done.4
  33.1 0.7 %prepare.1 = (bf16[256,512]{1,0:T(8,128)(2,1)S(1)}, bf16[50,960]{1,0:T(8,128)(2,1)S(1)}) custom-call(bf16[128,256]{1,0:T(8,128)(2,1)S(1)} %constants.1.after_ref.counter_ref, s32[4,128]{1,0:T(4,128)S(1)} %copy-done.6, f32[10,4,10]{2,1,0:T(4,128)S(1)} %bitcast.13), custom_call_target="tpu_custom_call" | custom-call | tf_op jit(solution)/shard_map/prepare/pallas_call | solution.py:34
  33.7 0.0 collective-permute-done.1.outer_ref
  33.8 0.0 collective-permute-done.inner_ref
  33.8 0.4 %beside.1 = (f32[50,50,128]{2,1,0:T(8,128)S(1)}, f32[100,128]{1,0:T(8,128)S(1)}, bf16[256,512]{1,0:T(8,128)(2,1)S(1)}) custom-call(f32[680,128]{1,0:T(8,128)S(1)} %collective-permute-done.inner_ref, f32[680,128]{1,0:T(8,128)S(1)} %collective-permute-done.1.outer_ref), custom_call_target="tpu_custom_call" | custom-call | tf_op jit(solution)/shard_map/beside/pallas_call | solution.py:34
  34.2 1.8 %collective-permute-done.6.outer_ref = f32[32,128]{1,0:T(8,128)S(1)} collective-permute-done((f32[32,128]{1,0:T(8,128)S(1)}, f32[32,128]{1,0:T(8,128)S(1)}, u32[]{:S(2)}, u32[]{:S(2)}) %collective-permute-start.6) | collective-permute-done | bytes 16416 | tf_op jit(solution)/shard_map/ppermute | solution.py:571
  36.0 0.0 collective-permute-done.7.inner_ref
  36.0 2.2 %sweeps.1 = (f32[50,128]{1,0:T(8,128)}, f32[50,128]{1,0:T(8,128)}) custom-call(f32[50,50,128]{2,1,0:T(8,128)S(1)} %copy-done, f32[50,50,128]{2,1,0:T(8,128)S(1)} %get-tuple-element.11.inverse_beside_ref, f32[50,128]{1,0:T(8,128)S(1)} %get-tuple-element.12.residual_ref, f32[64,128]{1,0:T(8,128)S(1)} %get-tuple-element.13.x_ref, ...), custom_call_target="tpu_custom_call" | custom-call | tf_op jit(solution)/shard_map/sweeps/pallas_call | solution.py:34
  (1 shorter events, 0.0 us)
Async XLA Ops:
  0.6 0.9 %copy-start.3 = (f32[35,5,256]{2,0,1:T(8,128)S(1)}, f32[35,5,256]{2,0,1:T(8,128)}, u32[]{:S(2)}) copy-start(f32[35,5,256]{2,0,1:T(8,128)} %param.10) | copy-start | bytes 537604
  0.6 0.9 %copy-start.5 = (f32[64,35]{0,1:T(8,128)S(1)}, f32[64,35]{0,1:T(8,128)}, u32[]{:S(2)}) copy-start(f32[64,35]{0,1:T(8,128)} %param.11) | copy-start | bytes 26884
  0.7 1.2 %copy-start.1 = (f32[64,10,256]{2,0,1:T(8,128)S(1)}, f32[64,10,256]{2,0,1:T(8,128)}, u32[]{:S(2)}) copy-start(f32[64,10,256]{2,0,1:T(8,128)} %param.12) | copy-start | bytes 1966084
  0.7 1.2 %copy-start.7 = (s32[256,4]{0,1:T(4,128)S(1)}, s32[256,4]{0,1:T(4,128)}, u32[]{:S(2)}) copy-start(s32[256,4]{0,1:T(4,128)} %param.14) | copy-start | bytes 12292
  0.7 1.2 %copy-start.8 = (s32[256,4]{0,1:T(4,128)S(1)}, s32[256,4]{0,1:T(4,128)}, u32[]{:S(2)}) copy-start(s32[256,4]{0,1:T(4,128)} %param.13) | copy-start | bytes 12292
  0.7 9.3 %copy-start = (f32[50,50,128]{2,1,0:T(8,128)S(1)}, f32[50,50,128]{2,1,0:T(8,128)}, u32[]{:S(2)}) copy-start(f32[50,50,128]{2,1,0:T(8,128)} %inverse_ref.7) | copy-start | bytes 3840004
  0.7 9.3 %copy-start.2 = (f32[4,5,5,128]{3,0,2,1:T(4,128)S(1)}, f32[4,5,5,128]{3,0,2,1:T(4,128)}, u32[]{:S(2)}) copy-start(f32[4,5,5,128]{3,0,2,1:T(4,128)} %param.17) | copy-start | bytes 153604
  0.7 9.3 %copy-start.6 = (s32[4,128]{1,0:T(4,128)S(1)}, s32[4,128]{1,0:T(4,128)}, u32[]{:S(2)}) copy-start(s32[4,128]{1,0:T(4,128)} %offset_ref.5) | copy-start | bytes 6148
  5.1 14.3 %all-to-all-start = ((f32[16,56,128]{2,1,0:T(8,128)}), f32[16,56,128]{2,1,0:T(8,128)S(1)}, u32[]{:S(2)}, u32[]{:S(2)}) async-start(f32[16,56,128]{2,1,0:T(8,128)} %restrict.1), calls=%async_computation | async-start | bytes 917504 | tf_op jit(solution)/shard_map/all_to_all | solution.py:509
  10.4 14.3 %copy-start.9 = (s32[128]{0:T(128)S(1)}, s32[128]{0:T(128)}, u32[]{:S(2)}) copy-start(s32[128]{0:T(128)} %param.15) | copy-start | bytes 1540
  10.8 22.3 %copy-start.4 = (f32[4,10,10]{2,0,1:T(4,128)S(1)}, f32[4,10,10]{2,0,1:T(4,128)}, u32[]{:S(2)}) copy-start(f32[4,10,10]{2,0,1:T(4,128)} %param.18) | copy-start | bytes 4804
  10.8 23.0 %collective-permute-start.1 = (f32[680,128]{1,0:T(8,128)S(1)}, f32[680,128]{1,0:T(8,128)S(1)}, u32[]{:S(2)}, u32[]{:S(2)}) collective-permute-start(f32[680,128]{1,0:T(8,128)S(1)} %pack_outer.1), channel_id=1, source_target_pairs={{1,2},{3,4},{5,6},{7,8},{9,10},{11,12},{13,14},{15,16},{17,18},{19... | collective-permute-start | bytes 1044488 | tf_op jit(solution)/shard_map/ppermute | solution.py:557
  15.0 18.7 %collective-permute-start = (f32[680,128]{1,0:T(8,128)S(1)}, f32[680,128]{1,0:T(8,128)S(1)}, u32[]{:S(2)}, u32[]{:S(2)}) collective-permute-start(f32[680,128]{1,0:T(8,128)S(1)} %pack_inner.1.after_ref), channel_id=1, source_target_pairs={{0,1},{1,0},{2,3},{3,2},{4,5},{5,4},{6,7},{7,6},{8,9},{9,8},{10,11... | collective-permute-start | bytes 1044488 | tf_op jit(solution)/shard_map/ppermute | solution.py:556
  19.8 4.9 %collective-permute-start.2 = (f32[50,128]{1,0:T(8,128)S(1)}, f32[50,128]{1,0:T(8,128)S(1)}, u32[]{:S(2)}, u32[]{:S(2)}) collective-permute-start(f32[50,128]{1,0:T(8,128)S(1)} %seat_far.1), channel_id=1, source_target_pairs={{0,16},{16,0},{1,17},{17,1},{2,18},{18,2},{3,19},{19,3},{4,20},{20... | collective-permute-start | bytes 76808 | tf_op jit(solution)/shard_map/ppermute | solution.py:50
  24.8 3.3 %collective-permute-start.3 = (f32[51,128]{1,0:T(8,128)S(1)}, f32[51,128]{1,0:T(8,128)S(1)}, u32[]{:S(2)}, u32[]{:S(2)}) collective-permute-start(f32[51,128]{1,0:T(8,128)S(1)} %renumber.1.refs_0_), channel_id=1, source_target_pairs={{0,3},{1,2},{2,1},{3,0},{4,7},{5,6},{6,5},{7,4},{8,11},{9,10},{10,... | collective-permute-start | bytes 78344 | tf_op jit(solution)/shard_map/ppermute | solution.py:50
  24.9 4.1 %collective-permute-start.4 = (f32[51,128]{1,0:T(8,128)S(1)}, f32[51,128]{1,0:T(8,128)S(1)}, u32[]{:S(2)}, u32[]{:S(2)}) collective-permute-start(f32[51,128]{1,0:T(8,128)S(1)} %renumber.1.refs_0_), channel_id=1, source_target_pairs={{0,2},{1,3},{2,0},{3,1},{4,6},{5,7},{6,4},{7,5},{8,10},{9,11},{10,... | collective-permute-start | bytes 78344 | tf_op jit(solution)/shard_map/ppermute | solution.py:50
  26.9 2.1 %collective-permute-start.5 = (f32[51,128]{1,0:T(8,128)S(1)}, f32[51,128]{1,0:T(8,128)S(1)}, u32[]{:S(2)}, u32[]{:S(2)}) collective-permute-start(f32[51,128]{1,0:T(8,128)S(1)} %renumber.1.refs_0_), channel_id=1, source_target_pairs={{0,1},{1,0},{2,3},{3,2},{4,5},{5,4},{6,7},{7,6},{8,9},{9,8},{10,11... | collective-permute-start | bytes 78344 | tf_op jit(solution)/shard_map/ppermute | solution.py:50
  29.2 6.9 %collective-permute-start.6 = (f32[32,128]{1,0:T(8,128)S(1)}, f32[32,128]{1,0:T(8,128)S(1)}, u32[]{:S(2)}, u32[]{:S(2)}) collective-permute-start(f32[32,128]{1,0:T(8,128)S(1)} %get-tuple-element.14), channel_id=1, source_target_pairs={{1,2},{3,4},{5,6},{7,8},{9,10},{11,12},{13,14},{15,16},{17,18},{19... | collective-permute-start | bytes 49160 | tf_op jit(solution)/shard_map/ppermute | solution.py:571
  31.1 4.9 %collective-permute-start.7 = (f32[32,128]{1,0:T(8,128)S(1)}, f32[32,128]{1,0:T(8,128)S(1)}, u32[]{:S(2)}, u32[]{:S(2)}) collective-permute-start(f32[32,128]{1,0:T(8,128)S(1)} %get-tuple-element.15), channel_id=1, source_target_pairs={{0,1},{1,0},{2,3},{3,2},{4,5},{5,4},{6,7},{7,6},{8,9},{9,8},{10,11... | collective-permute-start | bytes 49160 | tf_op jit(solution)/shard_map/ppermute | solution.py:572
